TPU v7x, 512 devices: a whole 4x4x16 slice. The times are simulated.
512 devices in a mesh: ia: 8 (over x, core), ja: 8 (over z_lo), ka: 8 (over z_hi, y).
Axes of the slice: x: 4, y: 4, z: 16 (z_hi: 2, z_lo: 8; z = z_hi * 8 + z_lo), core: 2. Of those that a mesh axis runs over, the one named last changes fastest.
Arguments:
- tokens: bfloat16 [2048, 4096], P('ia', ('ka', 'ja')), may hold values from -6 to 6
- weight_in: bfloat16 [4096, 16384], P('ka', ('ja', 'ia')), may hold values from -0.09375 to 0.09375
- weight_out: bfloat16 [16384, 4096], P('ja', ('ka', 'ia')), may hold values from -0.046875 to 0.046875
- cotangent: bfloat16 [2048, 4096], P('ia', ('ka', 'ja')), may hold values from -6 to 6
- row_mask: int32 [2048], P('ia'), may hold values 0 or 1
Outputs:
- block_out: bfloat16 [2048, 4096], P('ia', ('ka', 'ja'))
- grad_tokens: bfloat16 [2048, 4096], P('ia', ('ka', 'ja'))
All inputs are finite; a program needn't handle non-finite values. No bound on the sum of `row_mask` on one device may be relied on, other than what follows from the above.
Results may differ from a plain program's by a relative error of at most 0.02.
Values may be sent and summed in bfloat16 or wider, within the bound.
No kernel may reach another device: no remote copies, remote signals or barrier semaphores. Data moves between devices by JAX's collectives and lax.ppermute only.
A program may use at most 64 MiB of HBM per device.

v0:
```python
import jax
import jax.numpy as jnp
from jax import lax
from jax.sharding import PartitionSpec as P

gelu_coef = 0.7978845608028654


def gelu_value(preact):
    inner = gelu_coef * (preact + 0.044715 * preact * preact * preact)
    return 0.5 * preact * (1.0 + jnp.tanh(inner))


def gelu_slope(preact):
    inner = gelu_coef * (preact + 0.044715 * preact * preact * preact)
    tangent = jnp.tanh(inner)
    return 0.5 * (1.0 + tangent) + 0.5 * preact * (1.0 - tangent * tangent) * gelu_coef * (
        1.0 + 3.0 * 0.044715 * preact * preact
    )


def contract_last(left, right):
    return lax.dot_general(
        left, right, (((1,), (1,)), ((), ())), preferred_element_type=jnp.float32
    )


def shards(tokens, weight_in, weight_out, cotangent, row_mask):
    masked = cotangent * row_mask[:, None].astype(jnp.bfloat16)
    input_block, cot_block = (
        lax.all_gather(tokens, "ja", axis=1, tiled=True),
        lax.all_gather(masked, "ja", axis=1, tiled=True),
    )
    pre_terms = jnp.dot(
        input_block,
        lax.all_gather(weight_in, "ia", axis=1, tiled=True),
        preferred_element_type=jnp.float32,
    )
    columns = cot_block
    hidden_terms = contract_last(columns, lax.all_gather(weight_out, "ia", axis=1, tiled=True))
    preact = lax.psum_scatter(
        pre_terms.astype(jnp.bfloat16), "ka", scatter_dimension=1, tiled=True
    ).astype(jnp.float32)
    hidden_shard = gelu_value(preact).astype(jnp.bfloat16)
    hidden_block = lax.all_gather(hidden_shard, "ka", axis=1, tiled=True)
    out_terms = jnp.dot(
        hidden_block,
        lax.all_gather(weight_out, "ia", axis=1, tiled=True),
        preferred_element_type=jnp.float32,
    )
    branch = lax.psum_scatter(
        out_terms.astype(jnp.bfloat16), "ja", scatter_dimension=1, tiled=True
    ).astype(jnp.float32)
    grad_hidden = lax.psum_scatter(
        hidden_terms.astype(jnp.bfloat16), "ka", scatter_dimension=1, tiled=True
    ).astype(jnp.float32)
    grad_shard = (grad_hidden * gelu_slope(preact)).astype(jnp.bfloat16)
    grad_block = lax.all_gather(grad_shard, "ka", axis=1, tiled=True)
    columns = grad_block
    input_terms = contract_last(columns, lax.all_gather(weight_in, "ia", axis=1, tiled=True))
    grad_branch = lax.psum_scatter(
        input_terms.astype(jnp.bfloat16), "ja", scatter_dimension=1, tiled=True
    ).astype(jnp.float32)
    block_out = (tokens.astype(jnp.float32) + branch).astype(jnp.bfloat16)
    grad_tokens = (masked.astype(jnp.float32) + grad_branch).astype(jnp.bfloat16)
    return (block_out, grad_tokens)


def solution(mesh):
    return jax.shard_map(
        shards,
        mesh=mesh,
        in_specs=(
            P("ia", ("ka", "ja")),
            P("ka", ("ja", "ia")),
            P("ja", ("ka", "ia")),
            P("ia", ("ka", "ja")),
            P("ia"),
        ),
        out_specs=(P("ia", ("ka", "ja")), P("ia", ("ka", "ja"))),
        check_vma=False,
    )
```

profile of v0, /device:TPU:6, one launch (start us, length us, event | category | flops | bytes accessed | tf_op | source)
XLA Modules:
  0.0 614.0 jit_solution(16605138877819614025)
XLA Ops:
  7.2 0.0 all-gather.9.cloned.1.call-start
  7.2 0.7 all-gather.9.cloned.1.call-update
  7.9 0.0 all-gather.5.cloned.1.call-start
  7.9 0.7 all-gather.5.cloned.1.call-update
  8.6 0.0 reduce-scatter.9.cloned.1.call-start
  8.7 0.7 convert_element_type.53
  9.4 0.8 broadcast_multiply_fusion
  10.1 49.5 %all_gather.24 = bf16[256,512]{0,1:T(8,128)(2,1)S(1)} all-gather(bf16[256,64]{0,1:T(8,128)(2,1)S(1)} %broadcast_multiply_fusion), channel_id=1, replica_groups=mesh['ia'=8,'ja'=8,'ka'=8] {'ja'}, dimensions={1}, use_global_device_ids=true | all-gather | bytes 294912 | tf_op jit(solution)/shard_map/all_gather | solution.py:32
  59.6 0.0 copy-start.1
  59.6 0.0 all-gather.9.cloned.1.call-done
  59.6 3.3 convolution_convert_fusion
  63.0 0.0 reduce-scatter.9.cloned.1.call-update
  63.0 0.0 reduce-scatter.5.cloned.1.call-start
  63.0 0.0 copy-done.1
  63.1 47.0 %all_gather.20 = bf16[256,512]{0,1:T(8,128)(2,1)S(1)} all-gather(bf16[256,64]{0,1:T(8,128)(2,1)S(1)} %copy-done.1), channel_id=1, replica_groups=mesh['ia'=8,'ja'=8,'ka'=8] {'ja'}, dimensions={1}, use_global_device_ids=true | all-gather | bytes 294912 | tf_op jit(solution)/shard_map/all_gather | solution.py:31
  110.1 0.0 all-gather.5.cloned.1.call-done
  110.1 3.3 convolution_convert_fusion.1
  113.4 0.0 reduce-scatter.5.cloned.1.call-update
  113.5 0.0 all-gather.11.cloned.1.call-start
  113.5 95.1 %reduce-scatter.9.cloned.1.call-done = bf16[256,256]{1,0:T(8,128)(2,1)} async-done(((bf16[256,2048]{1,0:T(8,128)(2,1)}), bf16[256,256]{1,0:T(8,128)(2,1)}) %reduce-scatter.9.cloned.1.call-update) | async-done | bytes 131088 | tf_op jit(solution)/shard_map/reduce_scatter | solution.py:54
  208.6 114.4 %reduce-scatter.5.cloned.1.call-done = bf16[256,256]{1,0:T(8,128)(2,1)} async-done(((bf16[256,2048]{1,0:T(8,128)(2,1)}), bf16[256,256]{1,0:T(8,128)(2,1)}) %reduce-scatter.5.cloned.1.call-update) | async-done | bytes 131088 | tf_op jit(solution)/shard_map/reduce_scatter | solution.py:41
  323.0 1.9 fusion.7
  324.9 0.0 copy-start
  324.9 0.0 all-gather.11.cloned.1.call-update
  324.9 0.0 all-gather.7.cloned.1.call-start
  324.9 0.5 all-gather.7.cloned.1.call-update
  325.5 0.0 reduce-scatter.11.cloned.1.call-start
  325.5 79.8 %all-gather.11.cloned.1.call-done = bf16[256,2048]{1,0:T(8,128)(2,1)} async-done(((bf16[256,256]{1,0:T(8,128)(2,1)}), bf16[256,2048]{1,0:T(8,128)(2,1)}) %all-gather.11.cloned.1.call-update) | async-done | bytes 1048592 | tf_op jit(solution)/shard_map/all_gather | solution.py:58
  405.3 3.4 convolution_convert_fusion.2
  408.7 0.0 copy-start.2
  408.7 0.0 reduce-scatter.11.cloned.1.call-update
  408.7 0.0 reduce-scatter.7.cloned.1.call-start
  408.8 79.1 %all-gather.7.cloned.1.call-done = bf16[256,2048]{1,0:T(8,128)(2,1)} async-done(((bf16[256,256]{1,0:T(8,128)(2,1)}), bf16[256,2048]{1,0:T(8,128)(2,1)}) %all-gather.7.cloned.1.call-update) | async-done | bytes 1048592 | tf_op jit(solution)/shard_map/all_gather | solution.py:45
  487.9 0.0 copy-done
  487.9 2.7 convolution_convert_fusion.3
  490.5 0.0 reduce-scatter.7.cloned.1.call-update
  490.6 54.7 %reduce-scatter.11.cloned.1.call-done = bf16[256,64]{0,1:T(8,128)(2,1)} async-done(((bf16[256,512]{0,1:T(8,128)(2,1)}), bf16[256,64]{0,1:T(8,128)(2,1)}) %reduce-scatter.11.cloned.1.call-update) | async-done | bytes 32784 | tf_op jit(solution)/shard_map/reduce_scatter | solution.py:61
  545.2 0.0 copy-done.2
  545.2 1.4 add_convert_fusion
  546.6 59.2 %reduce-scatter.7.cloned.1.call-done = bf16[256,64]{0,1:T(8,128)(2,1)} async-done(((bf16[256,512]{0,1:T(8,128)(2,1)}), bf16[256,64]{0,1:T(8,128)(2,1)}) %reduce-scatter.7.cloned.1.call-update) | async-done | bytes 32784 | tf_op jit(solution)/shard_map/reduce_scatter | solution.py:51
  605.8 1.4 add_convert_fusion.1
Async XLA Ops:
  7.2 52.5 %all-gather.9.cloned.1.call-start = ((), (), s32[]{:S(2)}) async-start(), calls=%async_computation.7 | async-start | bytes 2359296 | tf_op jit(solution)/shard_map/all_gather | solution.py:48
  7.9 102.2 %all-gather.5.cloned.1.call-start = ((), (), s32[]{:S(2)}) async-start(), calls=%async_computation.4 | async-start | bytes 2359296 | tf_op jit(solution)/shard_map/all_gather | solution.py:36
  8.6 199.9 %reduce-scatter.9.cloned.1.call-start = ((), (), s32[]{:S(2)}) async-start(), calls=%async_computation.9 | async-start | bytes 1179648 | tf_op jit(solution)/shard_map/reduce_scatter | solution.py:54
  59.6 3.4 copy-start.1
  63.0 260.0 %reduce-scatter.5.cloned.1.call-start = ((), (), s32[]{:S(2)}) async-start(), calls=%async_computation.5 | async-start | bytes 1179648 | tf_op jit(solution)/shard_map/reduce_scatter | solution.py:41
  113.5 291.9 %all-gather.11.cloned.1.call-start = ((), (), s32[]{:S(2)}) async-start(), calls=%async_computation.10 | async-start | bytes 1179648 | tf_op jit(solution)/shard_map/all_gather | solution.py:58
  324.9 163.0 %copy-start = (bf16[2048,512]{0,1:T(8,128)(2,1)S(1)}, bf16[2048,512]{0,1:T(8,128)(2,1)}, u32[]{:S(2)}) copy-start(bf16[2048,512]{0,1:T(8,128)(2,1)} %all-gather.9.cloned.1.call-done) | copy-start | bytes 6291460
  324.9 163.0 %all-gather.7.cloned.1.call-start = ((), (), s32[]{:S(2)}) async-start(), calls=%async_computation.6 | async-start | bytes 1179648 | tf_op jit(solution)/shard_map/all_gather | solution.py:45
  325.5 219.8 %reduce-scatter.11.cloned.1.call-start = ((), (), s32[]{:S(2)}) async-start(), calls=%async_computation.11 | async-start | bytes 294912 | tf_op jit(solution)/shard_map/reduce_scatter | solution.py:61
  408.7 136.5 %copy-start.2 = (bf16[256,64]{0,1:T(8,128)(2,1)S(1)}, bf16[256,64]{0,1:T(8,128)(2,1)}, u32[]{:S(2)}) copy-start(bf16[256,64]{0,1:T(8,128)(2,1)} %param.8) | copy-start | bytes 98308
  408.7 197.1 %reduce-scatter.7.cloned.1.call-start = ((), (), s32[]{:S(2)}) async-start(), calls=%async_computation.8 | async-start | bytes 294912 | tf_op jit(solution)/shard_map/reduce_scatter | solution.py:51
Sparse Core Ops, SparseCore 0:
  10.1 35.9 all-gather.8
  48.2 35.9 all-gather.4
  88.7 119.7 reduce-scatter.8
  213.6 109.3 reduce-scatter.4
  325.9 79.3 all-gather.10
  408.2 79.5 all-gather.6
  490.6 54.5 reduce-scatter.10
  548.2 57.5 reduce-scatter.6
where the time goes:
time: 614 us
  waiting for transfers between devices  484 us (79%)
  blocking collectives  96.5 us (16%)
  between operations  14.1 us (2%)
  matrix products  12.7 us (2%)
    reduce_scatter x1, waiting for transfers between devices, shards(): lax.psum_scatter(pre_terms.astype(jnp.bfloat16), 'ka', scatter_dimension=...  114 us
    reduce_scatter x1, waiting for transfers between devices, shards(): lax.psum_scatter(hidden_terms.astype(jnp.bfloat16), 'ka', scatter_dimensi...  95.1 us
    all_gather x1, waiting for transfers between devices, shards(): grad_block = lax.all_gather(grad_shard, 'ka', axis=1, tiled=True)  79.8 us
    all_gather x1, waiting for transfers between devices, shards(): hidden_block = lax.all_gather(hidden_shard, 'ka', axis=1, tiled=True)  79.1 us
    reduce_scatter x1, waiting for transfers between devices, shards(): lax.psum_scatter(out_terms.astype(jnp.bfloat16), 'ja', scatter_dimension=...  59.2 us
    reduce_scatter x1, waiting for transfers between devices, shards(): lax.psum_scatter(input_terms.astype(jnp.bfloat16), 'ja', scatter_dimensio...  54.7 us
    all_gather x1, blocking collectives, shards(): lax.all_gather(masked, 'ja', axis=1, tiled=True)  49.5 us
    all_gather x1, blocking collectives, shards(): lax.all_gather(tokens, 'ja', axis=1, tiled=True)  47 us
  transfers between devices with their start and end apart: 8, of which 6 were waited for; matrix products, arithmetic and copies ran while one was open for 3% of the time, Pallas kernels for 0%

commit v1 on v0

v1 whole, which is shorter than its diff:
```python
import jax
import jax.numpy as jnp
from jax import lax
from jax.experimental import pallas as pl
from jax.experimental.pallas import tpu as pltpu
from jax.sharding import Mesh, PartitionSpec as P

gelu_coef = 0.7978845608028654

AXES = ("x", "core", "quad", "place", "half", "y")
SIZES = (4, 2, 2, 4, 2, 4)
IA, JA, KA = ("x", "core"), ("quad", "place"), ("half", "y")
QUADS = ("half", "quad")

VMEM = pl.BlockSpec(memory_space=pltpu.VMEM)
PARAMS = pltpu.CompilerParams(vmem_limit_bytes=48 * 2**20)


def exchange(parts, axis):
    return lax.all_to_all(parts, axis, split_axis=0, concat_axis=0, tiled=True)


def spread(shard, axis, size):
    return exchange(jnp.broadcast_to(shard[None], (size,) + shard.shape), axis)


def gelu_both(preact):
    inner = gelu_coef * (preact + 0.044715 * preact * preact * preact)
    tangent = jnp.tanh(inner)
    value = 0.5 * preact * (1.0 + tangent)
    slope = 0.5 * (1.0 + tangent) + 0.5 * preact * (1.0 - tangent * tangent) * gelu_coef * (
        1.0 + 3.0 * 0.044715 * preact * preact
    )
    return value, slope


def whole_in(weights):
    return jnp.concatenate(
        [
            jnp.concatenate([weights[core, x, half, 0] for x in range(4) for core in range(2)], axis=1)
            for half in range(2)
        ],
        axis=0,
    )


def whole_out(weights):
    return jnp.concatenate(
        [
            jnp.concatenate([weights[core, x, half, 1, 64 * q : 64 * q + 64] for q in range(8)], axis=1)
            for half in range(2)
            for x in range(4)
            for core in range(2)
        ],
        axis=0,
    )


def first_kernel(inputs, weights, terms):
    for which, whole in ((0, whole_in), (1, whole_out)):
        block = jnp.concatenate(
            [inputs[place, group, which] for group in range(4) for place in range(4)], axis=0
        )
        full = whole(weights)
        product = lax.dot_general(full, block, (((0,), (0,)), ((), ())), preferred_element_type=jnp.float32)
        for part in range(4):
            terms[part, which] = product[256 * part : 256 * part + 256].astype(jnp.bfloat16)


def middle_kernel(terms, hidden):
    preact = sum(terms[part, 0].astype(jnp.float32) for part in range(4))
    grad = sum(terms[part, 1].astype(jnp.float32) for part in range(4))
    value, slope = gelu_both(preact)
    value = value.astype(jnp.bfloat16)
    grad = (grad * slope).astype(jnp.bfloat16)
    for part in range(4):
        hidden[part, 0] = value
        hidden[part, 1] = grad


def second_kernel(hidden, weights, terms):
    for which, whole in ((0, whole_out), (1, whole_in)):
        block = jnp.concatenate([hidden[part, which] for part in range(4)], axis=0)
        product = jnp.dot(whole(weights), block, preferred_element_type=jnp.float32).astype(jnp.bfloat16)
        for group in range(4):
            for place in range(4):
                start = 256 * group + 64 * place
                terms[place, group, which] = product[start : start + 64]


def call(kernel, shape, *operands):
    return pl.pallas_call(
        kernel,
        out_shape=jax.ShapeDtypeStruct(shape, jnp.bfloat16),
        in_specs=[VMEM] * len(operands),
        out_specs=VMEM,
        compiler_params=PARAMS,
    )(*operands)


def shards(tokens, weight_in, weight_out, cotangent, row_mask):
    masked = cotangent * row_mask[:, None].astype(jnp.bfloat16)
    own = jnp.stack([tokens.T, masked.T])
    packed = jnp.stack(
        [
            weight_in.reshape(512, 2, 128).transpose(1, 0, 2),
            weight_out.T.reshape(64, 8, 2, 128).transpose(2, 1, 0, 3).reshape(2, 512, 128),
        ],
        axis=1,
    )
    weights = exchange(packed, "half")
    weights = spread(weights, "x", 4)
    weights = spread(weights, "core", 2)
    inputs = spread(own, QUADS, 4)
    inputs = spread(inputs, "place", 4)
    terms = call(first_kernel, (4, 2, 256, 256), inputs, weights)
    hidden = call(middle_kernel, (4, 2, 256, 256), exchange(terms, "y"))
    hidden = exchange(hidden, "y")
    terms = call(second_kernel, (4, 4, 2, 64, 256), hidden, weights)
    terms = exchange(terms, "place").astype(jnp.float32).sum(0).astype(jnp.bfloat16)
    terms = exchange(terms, QUADS).astype(jnp.float32).sum(0)
    outs = (own.astype(jnp.float32) + terms).astype(jnp.bfloat16)
    return outs[0].T, outs[1].T


def solution(mesh):
    return jax.shard_map(
        shards,
        mesh=Mesh(mesh.devices.reshape(SIZES), AXES),
        in_specs=(P(IA, KA + JA), P(KA, JA + IA), P(JA, KA + IA), P(IA, KA + JA), P(IA)),
        out_specs=(P(IA, KA + JA), P(IA, KA + JA)),
        check_vma=False,
    )
```

time: 614 us -> 231 us (0.38)
  waiting for transfers between devices: 484 us -> 30.7 us
  blocking collectives: 96.5 us -> 153 us
  starting transfers between devices: 0.32 us -> 30.8 us
  between operations: 14.1 us -> 0.78 us
  matrix products: 12.7 us -> 0 us
  Pallas kernels: 0 us -> 7.22 us
  local copies, waits for them, and re-layouts: 0.01 us -> 6.59 us
    reduce_scatter x4 -> x0, waiting for transfers between devices: 323 us -> none  [the longest x1 114 us: shards(): lax.psum_scatter(pre_terms.astype(jnp.bfloat16), 'ka', scatter_dimension=...]
    all_gather x4 -> x0, waiting for transfers between devices: 159 us -> none  [the longest x1 79.8 us: shards(): grad_block = lax.all_gather(grad_shard, 'ka', axis=1, tiled=True)]
    all_to_all x0 -> x7, blocking collectives: none -> 153 us  [exchange(): return lax.all_to_all(parts, axis, split_axis=0, concat_axis=0, tiled=True)]
    all_gather x2 -> x0, blocking collectives: 96.5 us -> none  [the longest x1 49.5 us: shards(): lax.all_gather(masked, 'ja', axis=1, tiled=True)]
    all_to_all x0 -> x2, starting transfers between devices: none -> 30.8 us  [exchange(): return lax.all_to_all(parts, axis, split_axis=0, concat_axis=0, tiled=True)]
    all_to_all x0 -> x2, waiting for transfers between devices: none -> 30.7 us  [exchange(): return lax.all_to_all(parts, axis, split_axis=0, concat_axis=0, tiled=True)]
    dot_general x4 -> x0, matrix products: 12.7 us -> none  [the longest x2 6.72 us: contract_last(): lax.dot_general(left, right, (((1,), (1,)), ((), ())), preferred_element_...]
    pallas_call x0 -> x3, Pallas kernels: none -> 7.22 us  [call(): pl.pallas_call(kernel, out_shape=jax.ShapeDtypeStruct(shape, jnp.bfloat16...]
  transfers between devices with their start and end apart: 8 -> 2, of which waited for: 6 -> 2; matrix products, arithmetic and copies ran while one was open for 3% -> 0% of each run, Pallas kernels for 0% -> 0%
where the time goes in v1:
time: 231 us; the launch traced here: 229 us
  blocking collectives  153 us (66%)
  starting transfers between devices  30.8 us (13%)
  waiting for transfers between devices  30.7 us (13%)
  Pallas kernels  7.22 us (3%)
  local copies, waits for them, and re-layouts  6.59 us (3%)
    all_to_all x7, blocking collectives, exchange(): return lax.all_to_all(parts, axis, split_axis=0, concat_axis=0, tiled=True)  153 us
    all_to_all x2, starting transfers between devices, exchange(): return lax.all_to_all(parts, axis, split_axis=0, concat_axis=0, tiled=True)  30.8 us
    all_to_all x2, waiting for transfers between devices, exchange(): return lax.all_to_all(parts, axis, split_axis=0, concat_axis=0, tiled=True)  30.7 us
    pallas_call x3, Pallas kernels, call(): pl.pallas_call(kernel, out_shape=jax.ShapeDtypeStruct(shape, jnp.bfloat16...  7.22 us
  transfers between devices with their start and end apart: 2, of which 2 were waited for; matrix products, arithmetic and copies ran while one was open for 0% of the time, Pallas kernels for 0%

profile of v1, /device:TPU:6, one launch (start us, length us, event | category | flops | bytes accessed | tf_op | source)
XLA Modules:
  0.0 229.3 jit_solution(8117459322553681607)
XLA Ops:
  0.6 0.0 copy-start.2
  0.6 0.0 copy-start.1
  0.7 0.0 copy-start
  0.7 1.1 copy.18
  1.8 1.1 reshape.17
  2.9 0.1 copy.19
  3.0 0.1 copy.20
  3.1 0.1 pad_maximum_fusion
  3.2 0.8 copy.21
  4.0 15.1 %all-to-all-start.2 = ((bf16[2,2,512,128]{2,3,1,0:T(8,128)(2,1)}), bf16[2,2,512,128]{2,3,1,0:T(8,128)(2,1)S(1)}, u32[]{:S(2)}, u32[]{:S(2)}) async-start(bf16[2,2,512,128]{2,3,1,0:T(8,128)(2,1)} %copy.21), calls=%async_computation.2 | async-start | bytes 1048576 | tf_op jit(solution)/shard_map/all_to_all | solution.py:20
  19.1 0.0 copy-done.2
  19.1 0.0 copy-done.1
  19.1 0.0 copy-done
  19.1 17.0 %all-to-all-done.2 = bf16[2,2,512,128]{2,3,1,0:T(8,128)(2,1)S(1)} async-done(((bf16[2,2,512,128]{2,3,1,0:T(8,128)(2,1)}), bf16[2,2,512,128]{2,3,1,0:T(8,128)(2,1)S(1)}, u32[]{:S(2)}, u32[]{:S(2)}) %all-to-all-start.2) | async-done | bytes 524320 | tf_op jit(solution)/shard_map/all_to_all | solution.py:20
  36.2 0.7 broadcast_in_dim.8
  36.9 15.7 %all-to-all-start = ((bf16[4,2,64,256]{3,2,1,0:T(8,128)(2,1)}), bf16[4,2,64,256]{3,2,1,0:T(8,128)(2,1)S(1)}, u32[]{:S(2)}, u32[]{:S(2)}) async-start(bf16[4,2,64,256]{3,2,1,0:T(8,128)(2,1)} %broadcast_in_dim.8), calls=%async_computation | async-start | bytes 524288 | tf_op jit(solution)/shard_map/all_to_all | solution.py:20
  52.6 0.3 copy.22
  52.9 13.7 %all-to-all-done = bf16[4,2,64,256]{3,2,1,0:T(8,128)(2,1)S(1)} async-done(((bf16[4,2,64,256]{3,2,1,0:T(8,128)(2,1)}), bf16[4,2,64,256]{3,2,1,0:T(8,128)(2,1)S(1)}, u32[]{:S(2)}, u32[]{:S(2)}) %all-to-all-start) | async-done | bytes 262176 | tf_op jit(solution)/shard_map/all_to_all | solution.py:20
  66.6 0.4 broadcast_in_dim.10
  67.0 21.7 %all_to_all.45 = bf16[4,2,2,512,128]{4,3,2,1,0:T(8,128)(2,1)S(1)} all-to-all(bf16[4,2,2,512,128]{4,3,2,1,0:T(8,128)(2,1)S(1)} %broadcast_in_dim.10), channel_id=1, replica_groups=mesh['x'=4,'core'=2,'quad'=2,'place'=4,'half'=2,'y'=4] {'x'}, dimensions={0} | all-to-all | bytes 4194304 | tf_op jit(solution)/shard_map/all_to_all | solution.py:20
  88.7 1.2 broadcast_in_dim.11
  89.9 8.2 %all_to_all.46.weights = bf16[2,4,2,2,512,128]{5,4,3,2,1,0:T(8,128)(2,1)} all-to-all(bf16[2,4,2,2,512,128]{5,4,3,2,1,0:T(8,128)(2,1)S(1)} %broadcast_in_dim.11), channel_id=1, replica_groups=mesh['x'=4,'core'=2,'quad'=2,'place'=4,'half'=2,'y'=4] {'core'}, dimensions={0} | all-to-all | bytes 8388608 | tf_op jit(solution)/shard_map/all_to_all | solution.py:20
  98.1 0.1 broadcast_in_dim.9
  98.2 41.0 %all_to_all.47.inputs = bf16[4,4,2,64,256]{4,3,2,1,0:T(8,128)(2,1)S(1)} all-to-all(bf16[4,4,2,64,256]{4,3,2,1,0:T(8,128)(2,1)S(1)} %broadcast_in_dim.9), channel_id=1, replica_groups=mesh['x'=4,'core'=2,'quad'=2,'place'=4,'half'=2,'y'=4] {'place'}, dimensions={0} | all-to-all | bytes 2097152 | tf_op jit(solution)/shard_map/all_to_all | solution.py:20
  139.2 3.5 %shard_map.68 = bf16[4,2,256,256]{3,2,1,0:T(8,128)(2,1)S(1)} custom-call(bf16[4,4,2,64,256]{4,3,2,1,0:T(8,128)(2,1)S(1)} %all_to_all.47.inputs, bf16[2,4,2,2,512,128]{5,4,3,2,1,0:T(8,128)(2,1)} %all_to_all.46.weights), custom_call_target="tpu_custom_call" | custom-call | tf_op jit(solution)/shard_map/pallas_call | solution.py:92
  142.7 18.6 %all_to_all.48.terms = bf16[4,2,256,256]{3,2,1,0:T(8,128)(2,1)S(1)} all-to-all(bf16[4,2,256,256]{3,2,1,0:T(8,128)(2,1)S(1)} %shard_map.68), channel_id=1, replica_groups=mesh['x'=4,'core'=2,'quad'=2,'place'=4,'half'=2,'y'=4] {'y'}, dimensions={0} | all-to-all | bytes 2097152 | tf_op jit(solution)/shard_map/all_to_all | solution.py:20
  161.3 0.3 shard_map.69
  161.6 15.9 %all_to_all.49.hidden = bf16[4,2,256,256]{3,2,1,0:T(8,128)(2,1)S(1)} all-to-all(bf16[4,2,256,256]{3,2,1,0:T(8,128)(2,1)S(1)} %shard_map.69), channel_id=1, replica_groups=mesh['x'=4,'core'=2,'quad'=2,'place'=4,'half'=2,'y'=4] {'y'}, dimensions={0} | all-to-all | bytes 2097152 | tf_op jit(solution)/shard_map/all_to_all | solution.py:20
  177.5 3.4 %shard_map.70 = bf16[4,4,2,64,256]{4,3,2,1,0:T(8,128)(2,1)S(1)} custom-call(bf16[4,2,256,256]{3,2,1,0:T(8,128)(2,1)S(1)} %all_to_all.49.hidden, bf16[2,4,2,2,512,128]{5,4,3,2,1,0:T(8,128)(2,1)} %all_to_all.46.weights), custom_call_target="tpu_custom_call" | custom-call | tf_op jit(solution)/shard_map/pallas_call | solution.py:92
  180.9 25.7 %all_to_all.50 = bf16[4,4,2,64,256]{4,3,2,1,0:T(8,128)(2,1)S(1)} all-to-all(bf16[4,4,2,64,256]{4,3,2,1,0:T(8,128)(2,1)S(1)} %shard_map.70), channel_id=1, replica_groups=mesh['x'=4,'core'=2,'quad'=2,'place'=4,'half'=2,'y'=4] {'place'}, dimensions={0} | all-to-all | bytes 2097152 | tf_op jit(solution)/shard_map/all_to_all | solution.py:20
  206.6 0.2 reduce_sum.21
  206.8 21.9 %all_to_all.51 = bf16[4,2,64,256]{3,2,1,0:T(8,128)(2,1)S(1)} all-to-all(bf16[4,2,64,256]{3,2,1,0:T(8,128)(2,1)S(1)} %reduce_sum.21), channel_id=1, replica_groups=mesh['x'=4,'core'=2,'quad'=2,'place'=4,'half'=2,'y'=4] {'half','quad'}, dimensions={0} | all-to-all | bytes 524288 | tf_op jit(solution)/shard_map/all_to_all | solution.py:20
  228.7 0.6 slice_bitcast_fusion
  (5 shorter events, 0.1 us)
Async XLA Ops:
  0.6 18.5 %copy-start.2 = (s32[256]{0:T(256)S(1)}, s32[256]{0:T(256)}, u32[]{:S(2)}) copy-start(s32[256]{0:T(256)} %param.9) | copy-start | bytes 3076
  0.6 18.5 %copy-start.1 = (bf16[256,64]{0,1:T(8,128)(2,1)S(1)}, bf16[256,64]{0,1:T(8,128)(2,1)}, u32[]{:S(2)}) copy-start(bf16[256,64]{0,1:T(8,128)(2,1)} %param.8) | copy-start | bytes 98308
  0.7 18.5 %copy-start = (bf16[256,64]{0,1:T(8,128)(2,1)S(1)}, bf16[256,64]{0,1:T(8,128)(2,1)}, u32[]{:S(2)}) copy-start(bf16[256,64]{0,1:T(8,128)(2,1)} %param.5) | copy-start | bytes 98308
  4.0 32.2 %all-to-all-start.2 = ((bf16[2,2,512,128]{2,3,1,0:T(8,128)(2,1)}), bf16[2,2,512,128]{2,3,1,0:T(8,128)(2,1)S(1)}, u32[]{:S(2)}, u32[]{:S(2)}) async-start(bf16[2,2,512,128]{2,3,1,0:T(8,128)(2,1)} %copy.21), calls=%async_computation.2 | async-start | bytes 1048576 | tf_op jit(solution)/shard_map/all_to_all | solution.py:20
  36.9 29.7 %all-to-all-start = ((bf16[4,2,64,256]{3,2,1,0:T(8,128)(2,1)}), bf16[4,2,64,256]{3,2,1,0:T(8,128)(2,1)S(1)}, u32[]{:S(2)}, u32[]{:S(2)}) async-start(bf16[4,2,64,256]{3,2,1,0:T(8,128)(2,1)} %broadcast_in_dim.8), calls=%async_computation | async-start | bytes 524288 | tf_op jit(solution)/shard_map/all_to_all | solution.py:20

commit v2 on v1

v2 whole, which is shorter than its diff:
```python
import jax
import jax.numpy as jnp
from jax import lax
from jax.experimental import pallas as pl
from jax.experimental.pallas import tpu as pltpu
from jax.sharding import Mesh, PartitionSpec as P

gelu_coef = 0.7978845608028654

AXES = ("x", "core", "quad", "place", "half", "y")
SIZES = (4, 2, 2, 4, 2, 4)
IA, JA, KA = ("x", "core"), ("quad", "place"), ("half", "y")
QUADS = ("half", "quad")
ALONG_Z = ("quad", "place", "half")

VMEM = pl.BlockSpec(memory_space=pltpu.VMEM)
SMEM = pl.BlockSpec(memory_space=pltpu.SMEM)
BF16, F32 = jnp.bfloat16, jnp.float32


def exchange(parts, axis):
    return lax.all_to_all(parts, axis, split_axis=0, concat_axis=0, tiled=True)


def spread(shard, axis, size):
    return exchange(jnp.broadcast_to(shard[None], (size,) + shard.shape), axis)


def swap(block, axis):
    return lax.ppermute(block, axis, [(0, 1), (1, 0)])


def along_z(block, distance):
    index = lambda z: (z % 8) * 2 + z // 8
    return lax.ppermute(block, ALONG_Z, [(index(z), index((z + distance) % 16)) for z in range(16)])


def gelu_both(preact):
    inner = gelu_coef * (preact + 0.044715 * preact * preact * preact)
    tangent = jnp.tanh(inner)
    value = 0.5 * preact * (1.0 + tangent)
    slope = 0.5 * (1.0 + tangent) + 0.5 * preact * (1.0 - tangent * tangent) * gelu_coef * (
        1.0 + 3.0 * 0.044715 * preact * preact
    )
    return value, slope


def fetch(refs, held, arrived):
    copies = [pltpu.make_async_copy(ref, to, arrived.at[i]) for i, (ref, to) in enumerate(zip(refs, held))]
    for copy in copies:
        copy.start()
    for copy in copies:
        copy.wait()


def pick_half(half, weight_in, weight_out, in_part, out_part):
    in_part[...] = weight_in[:, 128 * half : 128 * half + 128]
    for q in range(8):
        start = 256 * q + 128 * half
        out_part[64 * q : 64 * q + 64] = weight_out[:, start : start + 128]


def split_kernel(where, *refs):
    operands, (rows, up, down), held, arrived = refs[:5], refs[5:8], refs[8:13], refs[13]
    fetch(operands, held, arrived)
    tokens, cotangent, row_mask, weight_in, weight_out = held
    rows[0] = tokens[...]
    rows[1] = cotangent[...] * row_mask[...].astype(BF16)
    for half in range(2):

        @pl.when(where[0] == half)
        def _():
            pick_half(half, weight_in, weight_out, up.at[:512], up.at[512:1024])
            pick_half(1 - half, weight_in, weight_out, down.at[:512], down.at[512:1024])

    for out in (up, down):
        for which in range(2):
            for lanes in range(2):
                start = 1024 + 128 * which + 64 * lanes
                out[start : start + 64] = rows[which, :, 128 * lanes : 128 * lanes + 128]


def join_kernel(below, above, blocks, next_rows, last_rows):
    for x in range(4):
        blocks[x, :1024] = below[:1024]
        blocks[x, 1024:] = above[:1024]
    for out, came in ((next_rows, above), (last_rows, below)):
        for which in range(2):
            for lanes in range(2):
                start = 1024 + 128 * which + 64 * lanes
                out[which, :, 128 * lanes : 128 * lanes + 128] = came[start : start + 64]


def rows_kernel(where, same, ahead, behind, far_a, far_b, rows):
    blocks = [(offset, quad, block, quad) for offset, block in ((0, same), (1, ahead), (15, behind)) for quad in range(4)]
    blocks += [(2, 0, far_a, 0), (2, 1, far_a, 1), (14, 3, far_b, 0), (14, 0, far_b, 1)]
    for offset, quad, block, slot in blocks:
        start = lax.rem(where[1] + offset + 4 * quad, 16)
        for which in range(2):
            rows[which, pl.ds(pl.multiple_of(64 * start, 64), 64)] = block[slot, which]


def first_kernel(where, rows, blocks, core_blocks, weights, terms):
    half, core = lax.div(lax.rem(where[1] + 12, 16), 8), where[2]
    for block, at_core in ((blocks, core), (core_blocks, 1 - core)):
        for at, at_half in ((0, half), (1024, 1 - half)):
            for x in range(4):
                lanes = pl.ds(pl.multiple_of(256 * x + 128 * at_core, 128), 128)
                weights[0, pl.ds(pl.multiple_of(512 * at_half, 512), 512), lanes] = block[x, at : at + 512]
                part = pl.ds(pl.multiple_of(512 * at_half + 128 * x + 64 * at_core, 64), 64)
                for q in range(8):
                    start = at + 512 + 64 * q
                    weights[1, part, 128 * q : 128 * q + 128] = block[x, start : start + 64]
    for which in range(2):
        product = lax.dot_general(
            weights[which], rows[which], (((0,), (0,)), ((), ())), preferred_element_type=F32
        )
        for part in range(4):
            terms[part, which] = product[256 * part : 256 * part + 256].astype(BF16)


def middle_kernel(terms, hidden):
    preact = sum(terms[part, 0].astype(F32) for part in range(4))
    grad = sum(terms[part, 1].astype(F32) for part in range(4))
    value, slope = gelu_both(preact)
    value = value.astype(BF16)
    grad = (grad * slope).astype(BF16)
    for part in range(4):
        hidden[part, 0] = value
        hidden[part, 1] = grad


def second_kernel(where, hidden, weights, same, ahead, behind, far_a, far_b, rows):
    place = lax.rem(where[1], 4)
    for which in range(2):
        block = jnp.concatenate([hidden[part, which] for part in range(4)], axis=0)
        rows[which] = jnp.dot(weights[1 - which], block, preferred_element_type=F32).astype(BF16)
    for group in range(4):
        for which in range(2):
            for offset, out, slot in (
                (0, same, group),
                (1, ahead, group),
                (3, behind, group),
                (2, far_a if group < 2 else far_b, group % 2),
            ):
                at = lax.rem(place + offset, 4)
                out[slot, which] = rows[which, pl.ds(pl.multiple_of(256 * group + 64 * at, 64), 64)]


def call(kernel, shapes, *operands, scratch=(), space=VMEM, mib=20):
    return pl.pallas_call(
        kernel,
        out_shape=[jax.ShapeDtypeStruct(shape, BF16) for shape in shapes],
        in_specs=[SMEM if operand.dtype == jnp.int32 and operand.shape == (3,) else space for operand in operands],
        out_specs=[VMEM] * len(shapes),
        scratch_shapes=[pltpu.VMEM(shape, BF16) if isinstance(shape, tuple) else shape for shape in scratch],
        compiler_params=pltpu.CompilerParams(vmem_limit_bytes=mib * 2**20),
    )(*operands)


def shards(tokens, weight_in, weight_out, cotangent, row_mask):
    half = lax.axis_index("half")
    at_z = 8 * half + 4 * lax.axis_index("quad") + lax.axis_index("place")
    where = jnp.stack([half, at_z, lax.axis_index("core")]).astype(jnp.int32)
    weights = (weight_in, weight_out.T)
    operands = (tokens.T, cotangent.T, row_mask[None]) + weights
    held = lambda arrays: [pltpu.VMEM(a.shape, a.dtype) for a in arrays] + [pltpu.SemaphoreType.DMA((len(arrays),))]
    outside = pl.BlockSpec(memory_space=pl.ANY)
    own, up, down = call(
        split_kernel, [(2, 64, 256), (1280, 128), (1280, 128)], where, *operands,
        scratch=held(operands), space=outside, mib=60,
    )
    blocks, next_rows, last_rows = call(
        join_kernel, [(4, 2048, 128), (2, 64, 256), (2, 64, 256)], along_z(up, 4), along_z(down, -4)
    )
    blocks = exchange(blocks, "x")
    same = jnp.stack([own, next_rows, along_z(next_rows, -4), last_rows])
    behind, ahead = along_z(same, 1), along_z(same, -1)
    far_a, far_b = along_z(same[:2], -2), along_z(jnp.stack([last_rows, own]), 2)
    (rows,) = call(rows_kernel, [(2, 1024, 256)], where, same, ahead, behind, far_a, far_b)
    blocks, rows = lax.optimization_barrier((blocks, rows))
    core_blocks = swap(blocks, "core")
    weights, terms = call(
        first_kernel, [(2, 1024, 1024), (4, 2, 256, 256)], where, rows, blocks, core_blocks
    )
    (hidden,) = call(middle_kernel, [(4, 2, 256, 256)], exchange(terms, "y"))
    hidden = exchange(hidden, "y")
    whole, part = (4, 2, 64, 256), (2, 2, 64, 256)
    same, ahead, behind, far_a, far_b = call(
        second_kernel, [whole, whole, whole, part, part], where, hidden, weights, scratch=[(2, 1024, 256)]
    )
    sums = [along_z(ahead, 1), along_z(behind, -1), jnp.concatenate([along_z(far_a, 2), along_z(far_b, -2)])]
    terms = same.astype(F32) + sum(block.astype(F32) for block in sums)
    terms = exchange(terms.astype(BF16), QUADS).astype(F32).sum(0)
    outs = (own.astype(F32) + terms).astype(BF16)
    return outs[0].T, outs[1].T


def solution(mesh):
    return jax.shard_map(
        shards,
        mesh=Mesh(mesh.devices.reshape(SIZES), AXES),
        in_specs=(P(IA, KA + JA), P(KA, JA + IA), P(JA, KA + IA), P(IA, KA + JA), P(IA)),
        out_specs=(P(IA, KA + JA), P(IA, KA + JA)),
        check_vma=False,
    )
```

time: 231 us -> 179 us (0.77)
  blocking collectives: 153 us -> 56.2 us
  starting transfers between devices: 30.8 us -> 55.9 us
  waiting for transfers between devices: 30.7 us -> 53.4 us
  local copies, waits for them, and re-layouts: 6.59 us -> 1.97 us
    all_to_all x7 -> x3, blocking collectives: 153 us -> 56.2 us  [exchange(): return lax.all_to_all(parts, axis, split_axis=0, concat_axis=0, tiled=True)]
    ppermute x0 -> x12, waiting for transfers between devices: none -> 53.4 us  [the longest x11 49.2 us: along_z(): lax.ppermute(block, ALONG_Z, [(index(z), index((z + distance) % 16)) for...]
    ppermute x0 -> x12, starting transfers between devices: none -> 51 us  [the longest x11 49 us: along_z(): lax.ppermute(block, ALONG_Z, [(index(z), index((z + distance) % 16)) for...]
    all_to_all x2 -> x1, waiting for transfers between devices: 30.7 us -> 0.01 us  [exchange(): return lax.all_to_all(parts, axis, split_axis=0, concat_axis=0, tiled=True)]
    all_to_all x2 -> x1, starting transfers between devices: 30.8 us -> 4.9 us  [exchange(): return lax.all_to_all(parts, axis, split_axis=0, concat_axis=0, tiled=True)]
    broadcast_in_dim x4 -> x0, local copies, waits for them, and re-layouts: 2.41 us -> none  [spread(): return exchange(jnp.broadcast_to(shard[None], (size,) + shard.shape), axis)]
    pallas_call x3 -> x6, Pallas kernels: 7.22 us -> 8.7 us  [call(): pl.pallas_call(kernel, out_shape=[jax.ShapeDtypeStruct(shape, BF16) for s...]
  transfers between devices with their start and end apart: 2 -> 13, of which waited for: 2 -> 8; matrix products, arithmetic and copies ran while one was open for 0% -> 0% of each run, Pallas kernels for 0% -> 0%
where the time goes in v2:
time: 179 us; the launch traced here: 178 us
  blocking collectives  56.2 us (31%)
  starting transfers between devices  55.9 us (31%)
  waiting for transfers between devices  53.4 us (30%)
  Pallas kernels  8.7 us (5%)
  local copies, waits for them, and re-layouts  1.97 us (1%)
    all_to_all x3, blocking collectives, exchange(): return lax.all_to_all(parts, axis, split_axis=0, concat_axis=0, tiled=True)  56.2 us
    ppermute x11, waiting for transfers between devices, along_z(): lax.ppermute(block, ALONG_Z, [(index(z), index((z + distance) % 16)) for...  49.2 us
    ppermute x11, starting transfers between devices, along_z(): lax.ppermute(block, ALONG_Z, [(index(z), index((z + distance) % 16)) for...  49 us
    pallas_call x6, Pallas kernels, call(): pl.pallas_call(kernel, out_shape=[jax.ShapeDtypeStruct(shape, BF16) for s...  8.7 us
    all_to_all x1, starting transfers between devices, exchange(): return lax.all_to_all(parts, axis, split_axis=0, concat_axis=0, tiled=True)  4.9 us
    ppermute x1, waiting for transfers between devices, swap(): return lax.ppermute(block, axis, [(0, 1), (1, 0)])  4.13 us
  transfers between devices with their start and end apart: 13, of which 8 were waited for; matrix products, arithmetic and copies ran while one was open for 0% of the time, Pallas kernels for 0%

profile of v2, /device:TPU:6, one launch (start us, length us, event | category | flops | bytes accessed | tf_op | source)
XLA Modules:
  0.0 177.8 jit_solution(4100149947794705869)
XLA Ops:
  0.6 0.7 pad_add_fusion.where
  1.3 2.8 %shard_map.68 = (bf16[2,64,256]{2,1,0:T(8,128)(2,1)}, bf16[1280,128]{1,0:T(8,128)(2,1)}, bf16[1280,128]{1,0:T(8,128)(2,1)}) custom-call(s32[3]{0:T(128)} %pad_add_fusion.where, bf16[64,256]{1,0:T(8,128)(2,1)} %bitcast.27, bf16[64,256]{1,0:T(8,128)(2,1)} %bitcast.28, s32[1,256]{1,0:T(1,128)} %bitcast.29, bf16[512,256]{1,0:T(8,128)(2,1)} %refs_3_.1, ...), custom_call_target="tpu_custom_call" | custom-call | tf_op jit(solution)/shard_map/pallas_call | solution.py:151
  4.1 9.1 %collective-permute-start = (bf16[1280,128]{1,0:T(8,128)(2,1)}, bf16[1280,128]{1,0:T(8,128)(2,1)S(1)}, u32[]{:S(2)}, u32[]{:S(2)}) collective-permute-start(bf16[1280,128]{1,0:T(8,128)(2,1)} %get-tuple-element.18), channel_id=1, source_target_pairs={{0,32},{8,40},{16,48},{24,56},{32,4},{40,12},{48,20},{56,28},{4,36... | collective-permute-start | bytes 983048 | tf_op jit(solution)/shard_map/ppermute | solution.py:35
  13.2 5.6 %collective-permute-start.1 = (bf16[1280,128]{1,0:T(8,128)(2,1)}, bf16[1280,128]{1,0:T(8,128)(2,1)S(1)}, u32[]{:S(2)}, u32[]{:S(2)}) collective-permute-start(bf16[1280,128]{1,0:T(8,128)(2,1)} %get-tuple-element.19), channel_id=1, source_target_pairs={{0,36},{8,44},{16,52},{24,60},{32,0},{40,8},{48,16},{56,24},{4,32}... | collective-permute-start | bytes 983048 | tf_op jit(solution)/shard_map/ppermute | solution.py:35
  18.8 10.7 %collective-permute-done.below = bf16[1280,128]{1,0:T(8,128)(2,1)S(1)} collective-permute-done((bf16[1280,128]{1,0:T(8,128)(2,1)}, bf16[1280,128]{1,0:T(8,128)(2,1)S(1)}, u32[]{:S(2)}, u32[]{:S(2)}) %collective-permute-start) | collective-permute-done | bytes 327712 | tf_op jit(solution)/shard_map/ppermute | solution.py:35
  29.5 21.7 %collective-permute-done.1.above = bf16[1280,128]{1,0:T(8,128)(2,1)S(1)} collective-permute-done((bf16[1280,128]{1,0:T(8,128)(2,1)}, bf16[1280,128]{1,0:T(8,128)(2,1)S(1)}, u32[]{:S(2)}, u32[]{:S(2)}) %collective-permute-start.1) | collective-permute-done | bytes 327712 | tf_op jit(solution)/shard_map/ppermute | solution.py:35
  51.1 0.3 shard_map.69
  51.4 0.0 copy-start
  51.4 1.3 copy-done
  52.7 0.0 copy-start.2
  52.7 0.0 copy-start.1
  52.7 4.9 %all-to-all-start = ((bf16[4,2048,128]{2,1,0:T(8,128)(2,1)}), bf16[4,2048,128]{2,1,0:T(8,128)(2,1)S(1)}, u32[]{:S(2)}, u32[]{:S(2)}) async-start(bf16[4,2048,128]{2,1,0:T(8,128)(2,1)} %copy-done), calls=%async_computation | async-start | bytes 4194304 | tf_op jit(solution)/shard_map/all_to_all | solution.py:22
  57.6 4.4 %collective-permute-start.2 = (bf16[2,64,256]{2,1,0:T(8,128)(2,1)S(1)}, bf16[2,64,256]{2,1,0:T(8,128)(2,1)S(1)}, u32[]{:S(2)}, u32[]{:S(2)}) collective-permute-start(bf16[2,64,256]{2,1,0:T(8,128)(2,1)S(1)} %get-tuple-element.21), channel_id=1, source_target_pairs={{0,36},{8,44},{16,52},{24,60},{32,0},{40,8},{48,16},{56,24},{4,32}... | collective-permute-start | bytes 196616 | tf_op jit(solution)/shard_map/ppermute | solution.py:35
  62.0 5.7 %collective-permute-done.2 = bf16[2,64,256]{2,1,0:T(8,128)(2,1)S(1)} collective-permute-done((bf16[2,64,256]{2,1,0:T(8,128)(2,1)S(1)}, bf16[2,64,256]{2,1,0:T(8,128)(2,1)S(1)}, u32[]{:S(2)}, u32[]{:S(2)}) %collective-permute-start.2) | collective-permute-done | bytes 65568 | tf_op jit(solution)/shard_map/ppermute | solution.py:35
  67.7 0.0 copy-done.2
  67.7 1.9 %collective-permute-start.4 = (bf16[4,2,64,256]{3,2,1,0:T(8,128)(2,1)S(1)}, bf16[4,2,64,256]{3,2,1,0:T(8,128)(2,1)S(1)}, u32[]{:S(2)}, u32[]{:S(2)}) collective-permute-start(bf16[4,2,64,256]{3,2,1,0:T(8,128)(2,1)S(1)} %pad_maximum_fusion.same), channel_id=1, source_target_pairs={{0,8},{8,16},{16,24},{24,32},{32,40},{40,48},{48,56},{56,4},{4,12}... | collective-permute-start | bytes 786440 | tf_op jit(solution)/shard_map/ppermute | solution.py:35
  69.7 5.1 %collective-permute-start.3 = (bf16[4,2,64,256]{3,2,1,0:T(8,128)(2,1)S(1)}, bf16[4,2,64,256]{3,2,1,0:T(8,128)(2,1)S(1)}, u32[]{:S(2)}, u32[]{:S(2)}) collective-permute-start(bf16[4,2,64,256]{3,2,1,0:T(8,128)(2,1)S(1)} %pad_maximum_fusion.same), channel_id=1, source_target_pairs={{0,60},{8,0},{16,8},{24,16},{32,24},{40,32},{48,40},{56,48},{4,56}... | collective-permute-start | bytes 786440 | tf_op jit(solution)/shard_map/ppermute | solution.py:35
  74.8 1.9 %collective-permute-start.6 = (bf16[2,2,64,256]{3,2,1,0:T(8,128)(2,1)S(1)}, bf16[2,2,64,256]{3,2,1,0:T(8,128)(2,1)S(1)}, u32[]{:S(2)}, u32[]{:S(2)}) collective-permute-start(bf16[2,2,64,256]{3,2,1,0:T(8,128)(2,1)S(1)} %get-tuple-element.34), channel_id=1, source_target_pairs={{0,16},{8,24},{16,32},{24,40},{32,48},{40,56},{48,4},{56,12},{4,20... | collective-permute-start | bytes 393224 | tf_op jit(solution)/shard_map/ppermute | solution.py:35
  76.8 6.0 %collective-permute-start.5 = (bf16[2,2,64,256]{3,2,1,0:T(8,128)(2,1)S(1)}, bf16[2,2,64,256]{3,2,1,0:T(8,128)(2,1)S(1)}, u32[]{:S(2)}, u32[]{:S(2)}) collective-permute-start(bf16[2,2,64,256]{3,2,1,0:T(8,128)(2,1)S(1)} %get-tuple-element.35), channel_id=1, source_target_pairs={{0,52},{8,60},{16,0},{24,8},{32,16},{40,24},{48,32},{56,40},{4,48}... | collective-permute-start | bytes 393224 | tf_op jit(solution)/shard_map/ppermute | solution.py:35
  82.8 1.3 collective-permute-done.6.far_b
  84.1 4.7 %collective-permute-done.5.far_a = bf16[2,2,64,256]{3,2,1,0:T(8,128)(2,1)S(1)} collective-permute-done((bf16[2,2,64,256]{3,2,1,0:T(8,128)(2,1)S(1)}, bf16[2,2,64,256]{3,2,1,0:T(8,128)(2,1)S(1)}, u32[]{:S(2)}, u32[]{:S(2)}) %collective-permute-start.5) | collective-permute-done | bytes 131104 | tf_op jit(solution)/shard_map/ppermute | solution.py:35
  88.9 0.0 collective-permute-done.4.behind
  88.9 0.0 collective-permute-done.3.ahead
  88.9 0.0 copy-done.1
  88.9 0.6 shard_map.70.rows
  89.5 0.0 all-to-all-done.blocks
  89.5 1.9 %collective-permute-start.7 = (bf16[4,2048,128]{2,1,0:T(8,128)(2,1)S(1)}, bf16[4,2048,128]{2,1,0:T(8,128)(2,1)S(1)}, u32[]{:S(2)}, u32[]{:S(2)}) collective-permute-start(bf16[4,2048,128]{2,1,0:T(8,128)(2,1)S(1)} %all-to-all-done.blocks), channel_id=1, source_target_pairs={{0,64},{64,0},{1,65},{65,1},{2,66},{66,2},{3,67},{67,3},{4,68},{68... | collective-permute-start | bytes 6291464 | tf_op jit(solution)/shard_map/ppermute | solution.py:30
  91.4 4.1 %collective-permute-done.7.core_blocks = bf16[4,2048,128]{2,1,0:T(8,128)(2,1)S(1)} collective-permute-done((bf16[4,2048,128]{2,1,0:T(8,128)(2,1)S(1)}, bf16[4,2048,128]{2,1,0:T(8,128)(2,1)S(1)}, u32[]{:S(2)}, u32[]{:S(2)}) %collective-permute-start.7) | collective-permute-done | bytes 2097184 | tf_op jit(solution)/shard_map/ppermute | solution.py:30
  95.6 2.9 %shard_map.71 = (bf16[2,1024,1024]{2,1,0:T(8,128)(2,1)S(1)}, bf16[4,2,256,256]{3,2,1,0:T(8,128)(2,1)S(1)}) custom-call(s32[3]{0:T(128)S(1)} %copy-done.1, bf16[2,1024,256]{2,1,0:T(8,128)(2,1)S(1)} %shard_map.70.rows, bf16[4,2048,128]{2,1,0:T(8,128)(2,1)S(1)} %all-to-all-done.blocks, bf16[4,2048,128]{2,1,0:T(8,128)(2,1)S(1)} %collective-permute-done.7.core_blocks), custom_call_target="tpu_custom_call" | custom-call | tf_op jit(solution)/shard_map/pallas_call | solution.py:151
  98.5 19.7 %all_to_all.20.terms = bf16[4,2,256,256]{3,2,1,0:T(8,128)(2,1)S(1)} all-to-all(bf16[4,2,256,256]{3,2,1,0:T(8,128)(2,1)S(1)} %get-tuple-element.25), channel_id=1, replica_groups=mesh['x'=4,'core'=2,'quad'=2,'place'=4,'half'=2,'y'=4] {'y'}, dimensions={0} | all-to-all | bytes 2097152 | tf_op jit(solution)/shard_map/all_to_all | solution.py:22
  118.1 0.3 shard_map.72
  118.4 16.7 %all_to_all.21.hidden = bf16[4,2,256,256]{3,2,1,0:T(8,128)(2,1)S(1)} all-to-all(bf16[4,2,256,256]{3,2,1,0:T(8,128)(2,1)S(1)} %shard_map.72), channel_id=1, replica_groups=mesh['x'=4,'core'=2,'quad'=2,'place'=4,'half'=2,'y'=4] {'y'}, dimensions={0} | all-to-all | bytes 2097152 | tf_op jit(solution)/shard_map/all_to_all | solution.py:22
  135.1 1.8 %shard_map.73 = (bf16[4,2,64,256]{3,2,1,0:T(8,128)(2,1)S(1)}, bf16[4,2,64,256]{3,2,1,0:T(8,128)(2,1)S(1)}, bf16[4,2,64,256]{3,2,1,0:T(8,128)(2,1)S(1)}, bf16[2,2...) custom-call(s32[3]{0:T(128)S(1)} %copy-done.1, bf16[4,2,256,256]{3,2,1,0:T(8,128)(2,1)S(1)} %all_to_all.21.hidden, ...), custom_call_target="tpu_custom_call" | custom-call | tf_op jit(solution)/shard_map/pallas_call | solution.py:151
  136.9 2.3 %collective-permute-start.8 = (bf16[4,2,64,256]{3,2,1,0:T(8,128)(2,1)S(1)}, bf16[4,2,64,256]{3,2,1,0:T(8,128)(2,1)S(1)}, u32[]{:S(2)}, u32[]{:S(2)}) collective-permute-start(bf16[4,2,64,256]{3,2,1,0:T(8,128)(2,1)S(1)} %get-tuple-element.28), channel_id=1, source_target_pairs={{0,8},{8,16},{16,24},{24,32},{32,40},{40,48},{48,56},{56,4},{4,12}... | collective-permute-start | bytes 786440 | tf_op jit(solution)/shard_map/ppermute | solution.py:35
  139.3 4.7 %collective-permute-start.9 = (bf16[4,2,64,256]{3,2,1,0:T(8,128)(2,1)S(1)}, bf16[4,2,64,256]{3,2,1,0:T(8,128)(2,1)S(1)}, u32[]{:S(2)}, u32[]{:S(2)}) collective-permute-start(bf16[4,2,64,256]{3,2,1,0:T(8,128)(2,1)S(1)} %get-tuple-element.29), channel_id=1, source_target_pairs={{0,60},{8,0},{16,8},{24,16},{32,24},{40,32},{48,40},{56,48},{4,56}... | collective-permute-start | bytes 786440 | tf_op jit(solution)/shard_map/ppermute | solution.py:35
  144.0 4.2 %collective-permute-start.10 = (bf16[2,2,64,256]{3,2,1,0:T(8,128)(2,1)S(1)}, bf16[2,2,64,256]{3,2,1,0:T(8,128)(2,1)S(1)}, u32[]{:S(2)}, u32[]{:S(2)}) collective-permute-start(bf16[2,2,64,256]{3,2,1,0:T(8,128)(2,1)S(1)} %get-tuple-element.30), channel_id=1, source_target_pairs={{0,16},{8,24},{16,32},{24,40},{32,48},{40,56},{48,4},{56,12},{4,20... | collective-permute-start | bytes 393224 | tf_op jit(solution)/shard_map/ppermute | solution.py:35
  148.2 3.8 %collective-permute-start.11 = (bf16[2,2,64,256]{3,2,1,0:T(8,128)(2,1)S(1)}, bf16[2,2,64,256]{3,2,1,0:T(8,128)(2,1)S(1)}, u32[]{:S(2)}, u32[]{:S(2)}) collective-permute-start(bf16[2,2,64,256]{3,2,1,0:T(8,128)(2,1)S(1)} %get-tuple-element.31), channel_id=1, source_target_pairs={{0,52},{8,60},{16,0},{24,8},{32,16},{40,24},{48,32},{56,40},{4,48}... | collective-permute-start | bytes 393224 | tf_op jit(solution)/shard_map/ppermute | solution.py:35
  152.0 1.4 collective-permute-done.10
  153.3 3.8 %collective-permute-done.11 = bf16[2,2,64,256]{3,2,1,0:T(8,128)(2,1)S(1)} collective-permute-done((bf16[2,2,64,256]{3,2,1,0:T(8,128)(2,1)S(1)}, bf16[2,2,64,256]{3,2,1,0:T(8,128)(2,1)S(1)}, u32[]{:S(2)}, u32[]{:S(2)}) %collective-permute-start.11) | collective-permute-done | bytes 131104 | tf_op jit(solution)/shard_map/ppermute | solution.py:35
  157.1 0.0 collective-permute-done.8
  157.1 0.0 collective-permute-done.9
  157.1 0.1 add_convert_fusion
  157.3 19.8 %all_to_all.22 = bf16[4,2,64,256]{3,2,1,0:T(8,128)(2,1)S(1)} all-to-all(bf16[4,2,64,256]{3,2,1,0:T(8,128)(2,1)S(1)} %add_convert_fusion), channel_id=1, replica_groups=mesh['x'=4,'core'=2,'quad'=2,'place'=4,'half'=2,'y'=4] {'half','quad'}, dimensions={0} | all-to-all | bytes 524288 | tf_op jit(solution)/shard_map/all_to_all | solution.py:22
  177.2 0.6 slice_bitcast_fusion
  (4 shorter events, 0.1 us)
Async XLA Ops:
  4.1 25.4 %collective-permute-start = (bf16[1280,128]{1,0:T(8,128)(2,1)}, bf16[1280,128]{1,0:T(8,128)(2,1)S(1)}, u32[]{:S(2)}, u32[]{:S(2)}) collective-permute-start(bf16[1280,128]{1,0:T(8,128)(2,1)} %get-tuple-element.18), channel_id=1, source_target_pairs={{0,32},{8,40},{16,48},{24,56},{32,4},{40,12},{48,20},{56,28},{4,36... | collective-permute-start | bytes 983048 | tf_op jit(solution)/shard_map/ppermute | solution.py:35
  13.2 37.9 %collective-permute-start.1 = (bf16[1280,128]{1,0:T(8,128)(2,1)}, bf16[1280,128]{1,0:T(8,128)(2,1)S(1)}, u32[]{:S(2)}, u32[]{:S(2)}) collective-permute-start(bf16[1280,128]{1,0:T(8,128)(2,1)} %get-tuple-element.19), channel_id=1, source_target_pairs={{0,36},{8,44},{16,52},{24,60},{32,0},{40,8},{48,16},{56,24},{4,32}... | collective-permute-start | bytes 983048 | tf_op jit(solution)/shard_map/ppermute | solution.py:35
  51.4 1.3 copy-start
  52.7 15.0 %copy-start.2 = (bf16[2,64,256]{2,1,0:T(8,128)(2,1)S(1)}, bf16[2,64,256]{2,1,0:T(8,128)(2,1)}, u32[]{:S(2)}) copy-start(bf16[2,64,256]{2,1,0:T(8,128)(2,1)} %get-tuple-element.17) | copy-start | bytes 196612
  52.7 36.1 %copy-start.1 = (s32[3]{0:T(128)S(1)}, s32[3]{0:T(128)}, u32[]{:S(2)}) copy-start(s32[3]{0:T(128)} %pad_add_fusion.where) | copy-start | bytes 40
  52.7 36.8 %all-to-all-start = ((bf16[4,2048,128]{2,1,0:T(8,128)(2,1)}), bf16[4,2048,128]{2,1,0:T(8,128)(2,1)S(1)}, u32[]{:S(2)}, u32[]{:S(2)}) async-start(bf16[4,2048,128]{2,1,0:T(8,128)(2,1)} %copy-done), calls=%async_computation | async-start | bytes 4194304 | tf_op jit(solution)/shard_map/all_to_all | solution.py:22
  57.6 10.1 %collective-permute-start.2 = (bf16[2,64,256]{2,1,0:T(8,128)(2,1)S(1)}, bf16[2,64,256]{2,1,0:T(8,128)(2,1)S(1)}, u32[]{:S(2)}, u32[]{:S(2)}) collective-permute-start(bf16[2,64,256]{2,1,0:T(8,128)(2,1)S(1)} %get-tuple-element.21), channel_id=1, source_target_pairs={{0,36},{8,44},{16,52},{24,60},{32,0},{40,8},{48,16},{56,24},{4,32}... | collective-permute-start | bytes 196616 | tf_op jit(solution)/shard_map/ppermute | solution.py:35
  67.7 21.1 %collective-permute-start.4 = (bf16[4,2,64,256]{3,2,1,0:T(8,128)(2,1)S(1)}, bf16[4,2,64,256]{3,2,1,0:T(8,128)(2,1)S(1)}, u32[]{:S(2)}, u32[]{:S(2)}) collective-permute-start(bf16[4,2,64,256]{3,2,1,0:T(8,128)(2,1)S(1)} %pad_maximum_fusion.same), channel_id=1, source_target_pairs={{0,8},{8,16},{16,24},{24,32},{32,40},{40,48},{48,56},{56,4},{4,12}... | collective-permute-start | bytes 786440 | tf_op jit(solution)/shard_map/ppermute | solution.py:35
  69.7 19.2 %collective-permute-start.3 = (bf16[4,2,64,256]{3,2,1,0:T(8,128)(2,1)S(1)}, bf16[4,2,64,256]{3,2,1,0:T(8,128)(2,1)S(1)}, u32[]{:S(2)}, u32[]{:S(2)}) collective-permute-start(bf16[4,2,64,256]{3,2,1,0:T(8,128)(2,1)S(1)} %pad_maximum_fusion.same), channel_id=1, source_target_pairs={{0,60},{8,0},{16,8},{24,16},{32,24},{40,32},{48,40},{56,48},{4,56}... | collective-permute-start | bytes 786440 | tf_op jit(solution)/shard_map/ppermute | solution.py:35
  74.8 9.3 %collective-permute-start.6 = (bf16[2,2,64,256]{3,2,1,0:T(8,128)(2,1)S(1)}, bf16[2,2,64,256]{3,2,1,0:T(8,128)(2,1)S(1)}, u32[]{:S(2)}, u32[]{:S(2)}) collective-permute-start(bf16[2,2,64,256]{3,2,1,0:T(8,128)(2,1)S(1)} %get-tuple-element.34), channel_id=1, source_target_pairs={{0,16},{8,24},{16,32},{24,40},{32,48},{40,56},{48,4},{56,12},{4,20... | collective-permute-start | bytes 393224 | tf_op jit(solution)/shard_map/ppermute | solution.py:35
  76.8 12.1 %collective-permute-start.5 = (bf16[2,2,64,256]{3,2,1,0:T(8,128)(2,1)S(1)}, bf16[2,2,64,256]{3,2,1,0:T(8,128)(2,1)S(1)}, u32[]{:S(2)}, u32[]{:S(2)}) collective-permute-start(bf16[2,2,64,256]{3,2,1,0:T(8,128)(2,1)S(1)} %get-tuple-element.35), channel_id=1, source_target_pairs={{0,52},{8,60},{16,0},{24,8},{32,16},{40,24},{48,32},{56,40},{4,48}... | collective-permute-start | bytes 393224 | tf_op jit(solution)/shard_map/ppermute | solution.py:35
  89.5 6.1 %collective-permute-start.7 = (bf16[4,2048,128]{2,1,0:T(8,128)(2,1)S(1)}, bf16[4,2048,128]{2,1,0:T(8,128)(2,1)S(1)}, u32[]{:S(2)}, u32[]{:S(2)}) collective-permute-start(bf16[4,2048,128]{2,1,0:T(8,128)(2,1)S(1)} %all-to-all-done.blocks), channel_id=1, source_target_pairs={{0,64},{64,0},{1,65},{65,1},{2,66},{66,2},{3,67},{67,3},{4,68},{68... | collective-permute-start | bytes 6291464 | tf_op jit(solution)/shard_map/ppermute | solution.py:30
  136.9 20.2 %collective-permute-start.8 = (bf16[4,2,64,256]{3,2,1,0:T(8,128)(2,1)S(1)}, bf16[4,2,64,256]{3,2,1,0:T(8,128)(2,1)S(1)}, u32[]{:S(2)}, u32[]{:S(2)}) collective-permute-start(bf16[4,2,64,256]{3,2,1,0:T(8,128)(2,1)S(1)} %get-tuple-element.28), channel_id=1, source_target_pairs={{0,8},{8,16},{16,24},{24,32},{32,40},{40,48},{48,56},{56,4},{4,12}... | collective-permute-start | bytes 786440 | tf_op jit(solution)/shard_map/ppermute | solution.py:35
  139.3 17.8 %collective-permute-start.9 = (bf16[4,2,64,256]{3,2,1,0:T(8,128)(2,1)S(1)}, bf16[4,2,64,256]{3,2,1,0:T(8,128)(2,1)S(1)}, u32[]{:S(2)}, u32[]{:S(2)}) collective-permute-start(bf16[4,2,64,256]{3,2,1,0:T(8,128)(2,1)S(1)} %get-tuple-element.29), channel_id=1, source_target_pairs={{0,60},{8,0},{16,8},{24,16},{32,24},{40,32},{48,40},{56,48},{4,56}... | collective-permute-start | bytes 786440 | tf_op jit(solution)/shard_map/ppermute | solution.py:35
  144.0 9.3 %collective-permute-start.10 = (bf16[2,2,64,256]{3,2,1,0:T(8,128)(2,1)S(1)}, bf16[2,2,64,256]{3,2,1,0:T(8,128)(2,1)S(1)}, u32[]{:S(2)}, u32[]{:S(2)}) collective-permute-start(bf16[2,2,64,256]{3,2,1,0:T(8,128)(2,1)S(1)} %get-tuple-element.30), channel_id=1, source_target_pairs={{0,16},{8,24},{16,32},{24,40},{32,48},{40,56},{48,4},{56,12},{4,20... | collective-permute-start | bytes 393224 | tf_op jit(solution)/shard_map/ppermute | solution.py:35
  148.2 8.9 %collective-permute-start.11 = (bf16[2,2,64,256]{3,2,1,0:T(8,128)(2,1)S(1)}, bf16[2,2,64,256]{3,2,1,0:T(8,128)(2,1)S(1)}, u32[]{:S(2)}, u32[]{:S(2)}) collective-permute-start(bf16[2,2,64,256]{3,2,1,0:T(8,128)(2,1)S(1)} %get-tuple-element.31), channel_id=1, source_target_pairs={{0,52},{8,60},{16,0},{24,8},{32,16},{40,24},{48,32},{56,40},{4,48}... | collective-permute-start | bytes 393224 | tf_op jit(solution)/shard_map/ppermute | solution.py:35

commit v3 on v2

v3 whole, which is shorter than its diff:
```python
import jax
import jax.numpy as jnp
from jax import lax
from jax.experimental import pallas as pl
from jax.experimental.pallas import tpu as pltpu
from jax.sharding import Mesh, PartitionSpec as P

gelu_coef = 0.7978845608028654

AXES = ("x", "core", "quad", "place", "half", "y")
SIZES = (4, 2, 2, 4, 2, 4)
IA, JA, KA = ("x", "core"), ("quad", "place"), ("half", "y")
QUADS = ("half", "quad")
ALONG_Z = ("quad", "place", "half")

VMEM = pl.BlockSpec(memory_space=pltpu.VMEM)
BF16, F32 = jnp.bfloat16, jnp.float32
COST = 5 * 10**10


def exchange(parts, axis):
    return lax.all_to_all(parts, axis, split_axis=0, concat_axis=0, tiled=True)


def spread(shard, axis, size):
    return exchange(jnp.broadcast_to(shard[None], (size,) + shard.shape), axis)


def swap(block, axis):
    return lax.ppermute(block, axis, [(0, 1), (1, 0)])


def along_z(block, distance):
    index = lambda z: (z % 8) * 2 + z // 8
    return lax.ppermute(block, ALONG_Z, [(index(z), index((z + distance) % 16)) for z in range(16)])


def place_on_z():
    return 8 * lax.axis_index("half") + 4 * lax.axis_index("quad") + lax.axis_index("place")


def gelu_both(preact):
    inner = gelu_coef * (preact + 0.044715 * preact * preact * preact)
    tangent = jnp.tanh(inner)
    value = 0.5 * preact * (1.0 + tangent)
    slope = 0.5 * (1.0 + tangent) + 0.5 * preact * (1.0 - tangent * tangent) * gelu_coef * (
        1.0 + 3.0 * 0.044715 * preact * preact
    )
    return value, slope


def fetch(refs, held, arrived):
    copies = [pltpu.make_async_copy(ref, to, arrived.at[i]) for i, (ref, to) in enumerate(zip(refs, held))]
    for copy in copies:
        copy.start()
    for copy in copies:
        copy.wait()


def pick_half(half, weight_in, weight_out, in_part, out_part):
    in_part[...] = weight_in[:, 128 * half : 128 * half + 128]
    for q in range(8):
        start = 256 * q + 128 * half
        out_part[64 * q : 64 * q + 64] = weight_out[:, start : start + 128]


def split_kernel(*refs):
    operands, (rows, up, down), held, arrived = refs[:5], refs[5:8], refs[8:13], refs[13]
    fetch(operands, held, arrived)
    tokens, cotangent, row_mask, weight_in, weight_out = held
    rows[0] = tokens[...]
    rows[1] = cotangent[...] * row_mask[...].astype(BF16)
    for half in range(2):

        @pl.when(lax.axis_index("half") == half)
        def _():
            pick_half(half, weight_in, weight_out, up.at[:512], up.at[512:1024])
            pick_half(1 - half, weight_in, weight_out, down.at[:512], down.at[512:1024])

    for out in (up, down):
        for which in range(2):
            for lanes in range(2):
                start = 1024 + 128 * which + 64 * lanes
                out[start : start + 64] = rows[which, :, 128 * lanes : 128 * lanes + 128]


def join_kernel(below, above, blocks, next_rows, last_rows, moved):
    copies = []
    for x in range(4):
        for at, came in ((0, below), (1024, above)):
            copies.append(pltpu.make_async_copy(came.at[:1024], blocks.at[x, at : at + 1024], moved.at[len(copies)]))
    for out, came in ((next_rows, above), (last_rows, below)):
        for which in range(2):
            for lanes in range(2):
                start = 1024 + 128 * which + 64 * lanes
                part = out.at[which, :, 128 * lanes : 128 * lanes + 128]
                copies.append(pltpu.make_async_copy(came.at[start : start + 64], part, moved.at[len(copies)]))
    for copy in copies:
        copy.start()
    for copy in copies:
        copy.wait()


def lay_rows(rows, same, ahead, behind, far_a, far_b):
    at_z = place_on_z()
    blocks = [(offset, quad, block, quad) for offset, block in ((0, same), (1, ahead), (15, behind)) for quad in range(4)]
    blocks += [(2, 0, far_a, 0), (2, 1, far_a, 1), (14, 3, far_b, 0), (14, 0, far_b, 1)]
    for offset, quad, block, slot in blocks:
        start = lax.rem(at_z + offset + 4 * quad, 16)
        for which in range(2):
            rows[which, pl.ds(pl.multiple_of(64 * start, 64), 64)] = block[slot, which]


def lay_weights(weights, block, at_core):
    half = lax.div(lax.rem(place_on_z() + 12, 16), 8)
    for at, at_half in ((0, half), (1024, 1 - half)):
        for x in range(4):
            lanes = pl.ds(pl.multiple_of(256 * x + 128 * at_core, 128), 128)
            weights[0, pl.ds(pl.multiple_of(512 * at_half, 512), 512), lanes] = block[x, at : at + 512]
            part = pl.ds(pl.multiple_of(512 * at_half + 128 * x + 64 * at_core, 64), 64)
            for q in range(8):
                start = at + 512 + 64 * q
                weights[1, part, 128 * q : 128 * q + 128] = block[x, start : start + 64]


def own_kernel(same, ahead, behind, far_a, far_b, blocks, rows, weights):
    lay_rows(rows, same, ahead, behind, far_a, far_b)
    lay_weights(weights, blocks, lax.axis_index("core"))


def first_kernel(rows, begun, core_blocks, weights, terms):
    lay_weights(weights, core_blocks, 1 - lax.axis_index("core"))
    for which in range(2):
        product = lax.dot_general(
            rows[which], weights[which], (((0,), (0,)), ((), ())), preferred_element_type=F32
        )
        for part in range(4):
            terms[part, which] = product[:, 256 * part : 256 * part + 256].astype(BF16)


def middle_kernel(terms, hidden):
    preact = sum(terms[part, 0].astype(F32) for part in range(4))
    grad = sum(terms[part, 1].astype(F32) for part in range(4))
    value, slope = gelu_both(preact)
    value = value.astype(BF16)
    grad = (grad * slope).astype(BF16)
    for part in range(4):
        hidden[part, 0] = value
        hidden[part, 1] = grad


def second_kernel(hidden, weights, same, ahead, behind, far_a, far_b, rows):
    place = lax.axis_index("place")
    for which in range(2):
        block = jnp.concatenate([hidden[part, which] for part in range(4)], axis=1)
        product = lax.dot_general(
            weights[1 - which], block, (((1,), (1,)), ((), ())), preferred_element_type=F32
        )
        rows[which] = product.astype(BF16)
    for group in range(4):
        for which in range(2):
            for offset, out, slot in (
                (0, same, group),
                (1, ahead, group),
                (3, behind, group),
                (2, far_a if group < 2 else far_b, group % 2),
            ):
                at = lax.rem(place + offset, 4)
                out[slot, which] = rows[which, pl.ds(pl.multiple_of(256 * group + 64 * at, 64), 64)]


def call(kernel, shapes, *operands, scratch=(), space=VMEM, out_space=VMEM, mib=20, aliases={}, cost=None):
    return pl.pallas_call(
        kernel,
        out_shape=[jax.ShapeDtypeStruct(shape, BF16) for shape in shapes],
        in_specs=[space] * len(operands),
        out_specs=[out_space] * len(shapes),
        scratch_shapes=[pltpu.VMEM(shape, BF16) if isinstance(shape, tuple) else shape for shape in scratch],
        input_output_aliases=aliases,
        cost_estimate=pl.CostEstimate(flops=cost, bytes_accessed=0, transcendentals=0) if cost else None,
        compiler_params=pltpu.CompilerParams(vmem_limit_bytes=mib * 2**20),
    )(*operands)


def shards(tokens, weight_in, weight_out, cotangent, row_mask):
    weights = (weight_in, weight_out.T)
    operands = (tokens.T, cotangent.T, row_mask[None]) + weights
    held = lambda arrays: [pltpu.VMEM(a.shape, a.dtype) for a in arrays] + [pltpu.SemaphoreType.DMA((len(arrays),))]
    outside = pl.BlockSpec(memory_space=pl.ANY)
    own, up, down = call(
        split_kernel, [(2, 64, 256), (1280, 128), (1280, 128)], *operands,
        scratch=held(operands), space=outside, mib=60,
    )
    blocks, next_rows, last_rows = call(
        join_kernel, [(4, 2048, 128), (2, 64, 256), (2, 64, 256)], along_z(up, 4), along_z(down, -4),
        scratch=[pltpu.SemaphoreType.DMA((16,))], space=outside, out_space=outside,
    )
    blocks = exchange(blocks, "x")
    same = jnp.stack([own, next_rows, along_z(next_rows, -4), last_rows])
    behind, ahead = along_z(same, 1), along_z(same, -1)
    far_a, far_b = along_z(same[:2], -2), along_z(jnp.stack([last_rows, own]), 2)
    rows, begun = call(
        own_kernel, [(2, 1024, 256), (2, 1024, 1024)], same, ahead, behind, far_a, far_b, blocks, cost=COST
    )
    weights, terms = call(
        first_kernel,
        [(2, 1024, 1024), (4, 2, 256, 256)],
        rows, begun, swap(blocks, "core"),
        aliases={1: 0},
    )
    (hidden,) = call(middle_kernel, [(4, 2, 256, 256)], exchange(terms, "y"))
    hidden = exchange(hidden, "y")
    whole, part = (4, 2, 64, 256), (2, 2, 64, 256)
    same, ahead, behind, far_a, far_b = call(
        second_kernel, [whole, whole, whole, part, part], hidden, weights, scratch=[(2, 1024, 256)]
    )
    sums = [along_z(ahead, 1), along_z(behind, -1), jnp.concatenate([along_z(far_a, 2), along_z(far_b, -2)])]
    terms = same.astype(F32) + sum(block.astype(F32) for block in sums)
    terms = exchange(terms.astype(BF16), QUADS).astype(F32).sum(0)
    outs = (own.astype(F32) + terms).astype(BF16)
    return outs[0].T, outs[1].T


def solution(mesh):
    return jax.shard_map(
        shards,
        mesh=Mesh(mesh.devices.reshape(SIZES), AXES),
        in_specs=(P(IA, KA + JA), P(KA, JA + IA), P(JA, KA + IA), P(IA, KA + JA), P(IA)),
        out_specs=(P(IA, KA + JA), P(IA, KA + JA)),
        check_vma=False,
    )
```

time: 179 us -> 173 us (0.966)
  waiting for transfers between devices: 53.4 us -> 48.9 us
  Pallas kernels: 8.7 us -> 6.46 us
  blocking collectives: 56.2 us -> 58.1 us
    ppermute x1, waiting for transfers between devices: 4.13 us -> 0.01 us  [swap(): return lax.ppermute(block, axis, [(0, 1), (1, 0)])]
    pallas_call x6, Pallas kernels: 8.7 us -> 6.46 us  [call(): pl.pallas_call(kernel, out_shape=[jax.ShapeDtypeStruct(shape, BF16) for s...]
    all_to_all x3, blocking collectives: 56.2 us -> 58.1 us  [exchange(): return lax.all_to_all(parts, axis, split_axis=0, concat_axis=0, tiled=True)]
  transfers between devices with their start and end apart: 13 -> 13, of which waited for: 8 -> 6; matrix products, arithmetic and copies ran while one was open for 0% -> 0% of each run, Pallas kernels for 0% -> 0%
where the time goes in v3:
time: 173 us; the launch traced here: 172 us
  blocking collectives  58.1 us (34%)
  starting transfers between devices  55.9 us (32%)
  waiting for transfers between devices  48.9 us (28%)
  Pallas kernels  6.46 us (4%)
  local copies, waits for them, and re-layouts  1.96 us (1%)
    all_to_all x3, blocking collectives, exchange(): return lax.all_to_all(parts, axis, split_axis=0, concat_axis=0, tiled=True)  58.1 us
    ppermute x11, starting transfers between devices, along_z(): lax.ppermute(block, ALONG_Z, [(index(z), index((z + distance) % 16)) for...  49 us
    ppermute x11, waiting for transfers between devices, along_z(): lax.ppermute(block, ALONG_Z, [(index(z), index((z + distance) % 16)) for...  48.9 us
    pallas_call x6, Pallas kernels, call(): pl.pallas_call(kernel, out_shape=[jax.ShapeDtypeStruct(shape, BF16) for s...  6.46 us
    all_to_all x1, starting transfers between devices, exchange(): return lax.all_to_all(parts, axis, split_axis=0, concat_axis=0, tiled=True)  4.9 us
  transfers between devices with their start and end apart: 13, of which 6 were waited for; matrix products, arithmetic and copies ran while one was open for 0% of the time, Pallas kernels for 0%

profile of v3, /device:TPU:6, one launch (start us, length us, event | category | flops | bytes accessed | tf_op | source)
XLA Modules:
  0.0 172.3 jit_solution(12584107363620359893)
XLA Ops:
  0.6 2.1 %shard_map.68 = (bf16[2,64,256]{2,1,0:T(8,128)(2,1)}, bf16[1280,128]{1,0:T(8,128)(2,1)}, bf16[1280,128]{1,0:T(8,128)(2,1)}) custom-call(bf16[64,256]{1,0:T(8,128)(2,1)} %bitcast.24, bf16[64,256]{1,0:T(8,128)(2,1)} %bitcast.25, s32[1,256]{1,0:T(1,128)} %bitcast.26, bf16[512,256]{1,0:T(8,128)(2,1)} %refs_3_.1, bf16[64,2048]{1,0:T(8,128)(2,1)} %bitcast.22), custom_call_target="tpu_custom_call" | custom-call | tf_op jit(solution)/shard_map/pallas_call | solution.py:173
  2.8 9.1 %collective-permute-start = (bf16[1280,128]{1,0:T(8,128)(2,1)}, bf16[1280,128]{1,0:T(8,128)(2,1)S(1)}, u32[]{:S(2)}, u32[]{:S(2)}) collective-permute-start(bf16[1280,128]{1,0:T(8,128)(2,1)} %get-tuple-element.18), channel_id=1, source_target_pairs={{0,32},{8,40},{16,48},{24,56},{32,4},{40,12},{48,20},{56,28},{4,36... | collective-permute-start | bytes 983048 | tf_op jit(solution)/shard_map/ppermute | solution.py:35
  11.9 5.6 %collective-permute-start.1 = (bf16[1280,128]{1,0:T(8,128)(2,1)}, bf16[1280,128]{1,0:T(8,128)(2,1)S(1)}, u32[]{:S(2)}, u32[]{:S(2)}) collective-permute-start(bf16[1280,128]{1,0:T(8,128)(2,1)} %get-tuple-element.19), channel_id=1, source_target_pairs={{0,36},{8,44},{16,52},{24,60},{32,0},{40,8},{48,16},{56,24},{4,32}... | collective-permute-start | bytes 983048 | tf_op jit(solution)/shard_map/ppermute | solution.py:35
  17.4 10.7 %collective-permute-done.below = bf16[1280,128]{1,0:T(8,128)(2,1)S(1)} collective-permute-done((bf16[1280,128]{1,0:T(8,128)(2,1)}, bf16[1280,128]{1,0:T(8,128)(2,1)S(1)}, u32[]{:S(2)}, u32[]{:S(2)}) %collective-permute-start) | collective-permute-done | bytes 327712 | tf_op jit(solution)/shard_map/ppermute | solution.py:35
  28.1 21.7 %collective-permute-done.1.above = bf16[1280,128]{1,0:T(8,128)(2,1)S(1)} collective-permute-done((bf16[1280,128]{1,0:T(8,128)(2,1)}, bf16[1280,128]{1,0:T(8,128)(2,1)S(1)}, u32[]{:S(2)}, u32[]{:S(2)}) %collective-permute-start.1) | collective-permute-done | bytes 327712 | tf_op jit(solution)/shard_map/ppermute | solution.py:35
  49.8 0.3 shard_map.69
  50.1 0.0 copy-start
  50.1 1.3 copy-done
  51.5 0.0 copy-start.1
  51.5 4.9 %all-to-all-start = ((bf16[4,2048,128]{2,1,0:T(8,128)(2,1)}), bf16[4,2048,128]{2,1,0:T(8,128)(2,1)S(1)}, u32[]{:S(2)}, u32[]{:S(2)}) async-start(bf16[4,2048,128]{2,1,0:T(8,128)(2,1)} %copy-done), calls=%async_computation | async-start | bytes 4194304 | tf_op jit(solution)/shard_map/all_to_all | solution.py:22
  56.4 4.4 %collective-permute-start.2 = (bf16[2,64,256]{2,1,0:T(8,128)(2,1)S(1)}, bf16[2,64,256]{2,1,0:T(8,128)(2,1)S(1)}, u32[]{:S(2)}, u32[]{:S(2)}) collective-permute-start(bf16[2,64,256]{2,1,0:T(8,128)(2,1)S(1)} %get-tuple-element.20), channel_id=1, source_target_pairs={{0,36},{8,44},{16,52},{24,60},{32,0},{40,8},{48,16},{56,24},{4,32}... | collective-permute-start | bytes 196616 | tf_op jit(solution)/shard_map/ppermute | solution.py:35
  60.8 5.7 %collective-permute-done.2 = bf16[2,64,256]{2,1,0:T(8,128)(2,1)S(1)} collective-permute-done((bf16[2,64,256]{2,1,0:T(8,128)(2,1)S(1)}, bf16[2,64,256]{2,1,0:T(8,128)(2,1)S(1)}, u32[]{:S(2)}, u32[]{:S(2)}) %collective-permute-start.2) | collective-permute-done | bytes 65568 | tf_op jit(solution)/shard_map/ppermute | solution.py:35
  66.4 0.0 copy-done.1
  66.5 1.9 %collective-permute-start.4 = (bf16[4,2,64,256]{3,2,1,0:T(8,128)(2,1)S(1)}, bf16[4,2,64,256]{3,2,1,0:T(8,128)(2,1)S(1)}, u32[]{:S(2)}, u32[]{:S(2)}) collective-permute-start(bf16[4,2,64,256]{3,2,1,0:T(8,128)(2,1)S(1)} %pad_maximum_fusion.same), channel_id=1, source_target_pairs={{0,8},{8,16},{16,24},{24,32},{32,40},{40,48},{48,56},{56,4},{4,12}... | collective-permute-start | bytes 786440 | tf_op jit(solution)/shard_map/ppermute | solution.py:35
  68.4 5.1 %collective-permute-start.3 = (bf16[4,2,64,256]{3,2,1,0:T(8,128)(2,1)S(1)}, bf16[4,2,64,256]{3,2,1,0:T(8,128)(2,1)S(1)}, u32[]{:S(2)}, u32[]{:S(2)}) collective-permute-start(bf16[4,2,64,256]{3,2,1,0:T(8,128)(2,1)S(1)} %pad_maximum_fusion.same), channel_id=1, source_target_pairs={{0,60},{8,0},{16,8},{24,16},{32,24},{40,32},{48,40},{56,48},{4,56}... | collective-permute-start | bytes 786440 | tf_op jit(solution)/shard_map/ppermute | solution.py:35
  73.6 1.9 %collective-permute-start.6 = (bf16[2,2,64,256]{3,2,1,0:T(8,128)(2,1)S(1)}, bf16[2,2,64,256]{3,2,1,0:T(8,128)(2,1)S(1)}, u32[]{:S(2)}, u32[]{:S(2)}) collective-permute-start(bf16[2,2,64,256]{3,2,1,0:T(8,128)(2,1)S(1)} %get-tuple-element.34), channel_id=1, source_target_pairs={{0,16},{8,24},{16,32},{24,40},{32,48},{40,56},{48,4},{56,12},{4,20... | collective-permute-start | bytes 393224 | tf_op jit(solution)/shard_map/ppermute | solution.py:35
  75.5 6.0 %collective-permute-start.5 = (bf16[2,2,64,256]{3,2,1,0:T(8,128)(2,1)S(1)}, bf16[2,2,64,256]{3,2,1,0:T(8,128)(2,1)S(1)}, u32[]{:S(2)}, u32[]{:S(2)}) collective-permute-start(bf16[2,2,64,256]{3,2,1,0:T(8,128)(2,1)S(1)} %get-tuple-element.35), channel_id=1, source_target_pairs={{0,52},{8,60},{16,0},{24,8},{32,16},{40,24},{48,32},{56,40},{4,48}... | collective-permute-start | bytes 393224 | tf_op jit(solution)/shard_map/ppermute | solution.py:35
  81.5 0.0 all-to-all-done.blocks
  81.5 1.9 %collective-permute-start.7 = (bf16[4,2048,128]{2,1,0:T(8,128)(2,1)S(1)}, bf16[4,2048,128]{2,1,0:T(8,128)(2,1)S(1)}, u32[]{:S(2)}, u32[]{:S(2)}) collective-permute-start(bf16[4,2048,128]{2,1,0:T(8,128)(2,1)S(1)} %all-to-all-done.blocks), channel_id=1, source_target_pairs={{0,64},{64,0},{1,65},{65,1},{2,66},{66,2},{3,67},{67,3},{4,68},{68... | collective-permute-start | bytes 6291464 | tf_op jit(solution)/shard_map/ppermute | solution.py:30
  83.5 0.0 collective-permute-done.6.far_b
  83.5 4.1 %collective-permute-done.5.far_a = bf16[2,2,64,256]{3,2,1,0:T(8,128)(2,1)S(1)} collective-permute-done((bf16[2,2,64,256]{3,2,1,0:T(8,128)(2,1)S(1)}, bf16[2,2,64,256]{3,2,1,0:T(8,128)(2,1)S(1)}, u32[]{:S(2)}, u32[]{:S(2)}) %collective-permute-start.5) | collective-permute-done | bytes 131104 | tf_op jit(solution)/shard_map/ppermute | solution.py:35
  87.6 0.0 collective-permute-done.4.behind
  87.6 0.0 collective-permute-done.3.ahead
  87.6 0.6 shard_map.70
  88.2 0.0 collective-permute-done.7.core_blocks
  88.2 1.8 %shard_map.71 = (bf16[2,1024,1024]{2,1,0:T(8,128)(2,1)S(1)}, bf16[4,2,256,256]{3,2,1,0:T(8,128)(2,1)S(1)}) custom-call(bf16[2,1024,256]{2,1,0:T(8,128)(2,1)S(1)} %get-tuple-element.23.rows, bf16[2,1024,1024]{2,1,0:T(8,128)(2,1)S(1)} %get-tuple-element.24.begun, ...), custom_call_target="tpu_custom_call", output_to_operand_aliasing={{0}: (1, {})} | custom-call | tf_op jit(solution)/shard_map/pallas_call | solution.py:173
  90.0 19.1 %all_to_all.20.terms = bf16[4,2,256,256]{3,2,1,0:T(8,128)(2,1)S(1)} all-to-all(bf16[4,2,256,256]{3,2,1,0:T(8,128)(2,1)S(1)} %get-tuple-element.25), channel_id=1, replica_groups=mesh['x'=4,'core'=2,'quad'=2,'place'=4,'half'=2,'y'=4] {'y'}, dimensions={0} | all-to-all | bytes 2097152 | tf_op jit(solution)/shard_map/all_to_all | solution.py:22
  109.0 0.3 shard_map.72
  109.4 16.0 %all_to_all.21.hidden = bf16[4,2,256,256]{3,2,1,0:T(8,128)(2,1)S(1)} all-to-all(bf16[4,2,256,256]{3,2,1,0:T(8,128)(2,1)S(1)} %shard_map.72), channel_id=1, replica_groups=mesh['x'=4,'core'=2,'quad'=2,'place'=4,'half'=2,'y'=4] {'y'}, dimensions={0} | all-to-all | bytes 2097152 | tf_op jit(solution)/shard_map/all_to_all | solution.py:22
  125.4 1.3 shard_map.73
  126.7 1.9 %collective-permute-start.8 = (bf16[4,2,64,256]{3,2,1,0:T(8,128)(2,1)S(1)}, bf16[4,2,64,256]{3,2,1,0:T(8,128)(2,1)S(1)}, u32[]{:S(2)}, u32[]{:S(2)}) collective-permute-start(bf16[4,2,64,256]{3,2,1,0:T(8,128)(2,1)S(1)} %get-tuple-element.28), channel_id=1, source_target_pairs={{0,8},{8,16},{16,24},{24,32},{32,40},{40,48},{48,56},{56,4},{4,12}... | collective-permute-start | bytes 786440 | tf_op jit(solution)/shard_map/ppermute | solution.py:35
  128.6 5.1 %collective-permute-start.9 = (bf16[4,2,64,256]{3,2,1,0:T(8,128)(2,1)S(1)}, bf16[4,2,64,256]{3,2,1,0:T(8,128)(2,1)S(1)}, u32[]{:S(2)}, u32[]{:S(2)}) collective-permute-start(bf16[4,2,64,256]{3,2,1,0:T(8,128)(2,1)S(1)} %get-tuple-element.29), channel_id=1, source_target_pairs={{0,60},{8,0},{16,8},{24,16},{32,24},{40,32},{48,40},{56,48},{4,56}... | collective-permute-start | bytes 786440 | tf_op jit(solution)/shard_map/ppermute | solution.py:35
  133.8 1.9 %collective-permute-start.10 = (bf16[2,2,64,256]{3,2,1,0:T(8,128)(2,1)S(1)}, bf16[2,2,64,256]{3,2,1,0:T(8,128)(2,1)S(1)}, u32[]{:S(2)}, u32[]{:S(2)}) collective-permute-start(bf16[2,2,64,256]{3,2,1,0:T(8,128)(2,1)S(1)} %get-tuple-element.30), channel_id=1, source_target_pairs={{0,16},{8,24},{16,32},{24,40},{32,48},{40,56},{48,4},{56,12},{4,20... | collective-permute-start | bytes 393224 | tf_op jit(solution)/shard_map/ppermute | solution.py:35
  135.7 6.0 %collective-permute-start.11 = (bf16[2,2,64,256]{3,2,1,0:T(8,128)(2,1)S(1)}, bf16[2,2,64,256]{3,2,1,0:T(8,128)(2,1)S(1)}, u32[]{:S(2)}, u32[]{:S(2)}) collective-permute-start(bf16[2,2,64,256]{3,2,1,0:T(8,128)(2,1)S(1)} %get-tuple-element.31), channel_id=1, source_target_pairs={{0,52},{8,60},{16,0},{24,8},{32,16},{40,24},{48,32},{56,40},{4,48}... | collective-permute-start | bytes 393224 | tf_op jit(solution)/shard_map/ppermute | solution.py:35
  141.7 1.0 collective-permute-done.10
  142.7 5.7 %collective-permute-done.11 = bf16[2,2,64,256]{3,2,1,0:T(8,128)(2,1)S(1)} collective-permute-done((bf16[2,2,64,256]{3,2,1,0:T(8,128)(2,1)S(1)}, bf16[2,2,64,256]{3,2,1,0:T(8,128)(2,1)S(1)}, u32[]{:S(2)}, u32[]{:S(2)}) %collective-permute-start.11) | collective-permute-done | bytes 131104 | tf_op jit(solution)/shard_map/ppermute | solution.py:35
  148.4 0.0 collective-permute-done.8
  148.5 0.0 collective-permute-done.9
  148.5 0.1 add_convert_fusion
  148.6 23.0 %all_to_all.22 = bf16[4,2,64,256]{3,2,1,0:T(8,128)(2,1)S(1)} all-to-all(bf16[4,2,64,256]{3,2,1,0:T(8,128)(2,1)S(1)} %add_convert_fusion), channel_id=1, replica_groups=mesh['x'=4,'core'=2,'quad'=2,'place'=4,'half'=2,'y'=4] {'half','quad'}, dimensions={0} | all-to-all | bytes 524288 | tf_op jit(solution)/shard_map/all_to_all | solution.py:22
  171.7 0.6 slice_bitcast_fusion
  (4 shorter events, 0.1 us)
Async XLA Ops:
  2.8 25.4 %collective-permute-start = (bf16[1280,128]{1,0:T(8,128)(2,1)}, bf16[1280,128]{1,0:T(8,128)(2,1)S(1)}, u32[]{:S(2)}, u32[]{:S(2)}) collective-permute-start(bf16[1280,128]{1,0:T(8,128)(2,1)} %get-tuple-element.18), channel_id=1, source_target_pairs={{0,32},{8,40},{16,48},{24,56},{32,4},{40,12},{48,20},{56,28},{4,36... | collective-permute-start | bytes 983048 | tf_op jit(solution)/shard_map/ppermute | solution.py:35
  11.9 37.9 %collective-permute-start.1 = (bf16[1280,128]{1,0:T(8,128)(2,1)}, bf16[1280,128]{1,0:T(8,128)(2,1)S(1)}, u32[]{:S(2)}, u32[]{:S(2)}) collective-permute-start(bf16[1280,128]{1,0:T(8,128)(2,1)} %get-tuple-element.19), channel_id=1, source_target_pairs={{0,36},{8,44},{16,52},{24,60},{32,0},{40,8},{48,16},{56,24},{4,32}... | collective-permute-start | bytes 983048 | tf_op jit(solution)/shard_map/ppermute | solution.py:35
  50.1 1.3 copy-start
  51.5 15.0 %copy-start.1 = (bf16[2,64,256]{2,1,0:T(8,128)(2,1)S(1)}, bf16[2,64,256]{2,1,0:T(8,128)(2,1)}, u32[]{:S(2)}) copy-start(bf16[2,64,256]{2,1,0:T(8,128)(2,1)} %get-tuple-element.17) | copy-start | bytes 196612
  51.5 30.1 %all-to-all-start = ((bf16[4,2048,128]{2,1,0:T(8,128)(2,1)}), bf16[4,2048,128]{2,1,0:T(8,128)(2,1)S(1)}, u32[]{:S(2)}, u32[]{:S(2)}) async-start(bf16[4,2048,128]{2,1,0:T(8,128)(2,1)} %copy-done), calls=%async_computation | async-start | bytes 4194304 | tf_op jit(solution)/shard_map/all_to_all | solution.py:22
  56.4 10.1 %collective-permute-start.2 = (bf16[2,64,256]{2,1,0:T(8,128)(2,1)S(1)}, bf16[2,64,256]{2,1,0:T(8,128)(2,1)S(1)}, u32[]{:S(2)}, u32[]{:S(2)}) collective-permute-start(bf16[2,64,256]{2,1,0:T(8,128)(2,1)S(1)} %get-tuple-element.20), channel_id=1, source_target_pairs={{0,36},{8,44},{16,52},{24,60},{32,0},{40,8},{48,16},{56,24},{4,32}... | collective-permute-start | bytes 196616 | tf_op jit(solution)/shard_map/ppermute | solution.py:35
  66.5 21.1 %collective-permute-start.4 = (bf16[4,2,64,256]{3,2,1,0:T(8,128)(2,1)S(1)}, bf16[4,2,64,256]{3,2,1,0:T(8,128)(2,1)S(1)}, u32[]{:S(2)}, u32[]{:S(2)}) collective-permute-start(bf16[4,2,64,256]{3,2,1,0:T(8,128)(2,1)S(1)} %pad_maximum_fusion.same), channel_id=1, source_target_pairs={{0,8},{8,16},{16,24},{24,32},{32,40},{40,48},{48,56},{56,4},{4,12}... | collective-permute-start | bytes 786440 | tf_op jit(solution)/shard_map/ppermute | solution.py:35
  68.4 19.2 %collective-permute-start.3 = (bf16[4,2,64,256]{3,2,1,0:T(8,128)(2,1)S(1)}, bf16[4,2,64,256]{3,2,1,0:T(8,128)(2,1)S(1)}, u32[]{:S(2)}, u32[]{:S(2)}) collective-permute-start(bf16[4,2,64,256]{3,2,1,0:T(8,128)(2,1)S(1)} %pad_maximum_fusion.same), channel_id=1, source_target_pairs={{0,60},{8,0},{16,8},{24,16},{32,24},{40,32},{48,40},{56,48},{4,56}... | collective-permute-start | bytes 786440 | tf_op jit(solution)/shard_map/ppermute | solution.py:35
  73.6 9.9 %collective-permute-start.6 = (bf16[2,2,64,256]{3,2,1,0:T(8,128)(2,1)S(1)}, bf16[2,2,64,256]{3,2,1,0:T(8,128)(2,1)S(1)}, u32[]{:S(2)}, u32[]{:S(2)}) collective-permute-start(bf16[2,2,64,256]{3,2,1,0:T(8,128)(2,1)S(1)} %get-tuple-element.34), channel_id=1, source_target_pairs={{0,16},{8,24},{16,32},{24,40},{32,48},{40,56},{48,4},{56,12},{4,20... | collective-permute-start | bytes 393224 | tf_op jit(solution)/shard_map/ppermute | solution.py:35
  75.5 12.1 %collective-permute-start.5 = (bf16[2,2,64,256]{3,2,1,0:T(8,128)(2,1)S(1)}, bf16[2,2,64,256]{3,2,1,0:T(8,128)(2,1)S(1)}, u32[]{:S(2)}, u32[]{:S(2)}) collective-permute-start(bf16[2,2,64,256]{3,2,1,0:T(8,128)(2,1)S(1)} %get-tuple-element.35), channel_id=1, source_target_pairs={{0,52},{8,60},{16,0},{24,8},{32,16},{40,24},{48,32},{56,40},{4,48}... | collective-permute-start | bytes 393224 | tf_op jit(solution)/shard_map/ppermute | solution.py:35
  81.5 6.7 %collective-permute-start.7 = (bf16[4,2048,128]{2,1,0:T(8,128)(2,1)S(1)}, bf16[4,2048,128]{2,1,0:T(8,128)(2,1)S(1)}, u32[]{:S(2)}, u32[]{:S(2)}) collective-permute-start(bf16[4,2048,128]{2,1,0:T(8,128)(2,1)S(1)} %all-to-all-done.blocks), channel_id=1, source_target_pairs={{0,64},{64,0},{1,65},{65,1},{2,66},{66,2},{3,67},{67,3},{4,68},{68... | collective-permute-start | bytes 6291464 | tf_op jit(solution)/shard_map/ppermute | solution.py:30
  126.7 21.8 %collective-permute-start.8 = (bf16[4,2,64,256]{3,2,1,0:T(8,128)(2,1)S(1)}, bf16[4,2,64,256]{3,2,1,0:T(8,128)(2,1)S(1)}, u32[]{:S(2)}, u32[]{:S(2)}) collective-permute-start(bf16[4,2,64,256]{3,2,1,0:T(8,128)(2,1)S(1)} %get-tuple-element.28), channel_id=1, source_target_pairs={{0,8},{8,16},{16,24},{24,32},{32,40},{40,48},{48,56},{56,4},{4,12}... | collective-permute-start | bytes 786440 | tf_op jit(solution)/shard_map/ppermute | solution.py:35
  128.6 19.8 %collective-permute-start.9 = (bf16[4,2,64,256]{3,2,1,0:T(8,128)(2,1)S(1)}, bf16[4,2,64,256]{3,2,1,0:T(8,128)(2,1)S(1)}, u32[]{:S(2)}, u32[]{:S(2)}) collective-permute-start(bf16[4,2,64,256]{3,2,1,0:T(8,128)(2,1)S(1)} %get-tuple-element.29), channel_id=1, source_target_pairs={{0,60},{8,0},{16,8},{24,16},{32,24},{40,32},{48,40},{56,48},{4,56}... | collective-permute-start | bytes 786440 | tf_op jit(solution)/shard_map/ppermute | solution.py:35
  133.8 9.0 %collective-permute-start.10 = (bf16[2,2,64,256]{3,2,1,0:T(8,128)(2,1)S(1)}, bf16[2,2,64,256]{3,2,1,0:T(8,128)(2,1)S(1)}, u32[]{:S(2)}, u32[]{:S(2)}) collective-permute-start(bf16[2,2,64,256]{3,2,1,0:T(8,128)(2,1)S(1)} %get-tuple-element.30), channel_id=1, source_target_pairs={{0,16},{8,24},{16,32},{24,40},{32,48},{40,56},{48,4},{56,12},{4,20... | collective-permute-start | bytes 393224 | tf_op jit(solution)/shard_map/ppermute | solution.py:35
  135.7 12.8 %collective-permute-start.11 = (bf16[2,2,64,256]{3,2,1,0:T(8,128)(2,1)S(1)}, bf16[2,2,64,256]{3,2,1,0:T(8,128)(2,1)S(1)}, u32[]{:S(2)}, u32[]{:S(2)}) collective-permute-start(bf16[2,2,64,256]{3,2,1,0:T(8,128)(2,1)S(1)} %get-tuple-element.31), channel_id=1, source_target_pairs={{0,52},{8,60},{16,0},{24,8},{32,16},{40,24},{48,32},{56,40},{4,48}... | collective-permute-start | bytes 393224 | tf_op jit(solution)/shard_map/ppermute | solution.py:35

commit v4 on v3

--- a/solution.py
+++ b/solution.py
@@ -101,14 +101,13 @@
         copy.wait()
 
 
-def lay_rows(rows, same, ahead, behind, far_a, far_b):
+def lay_rows(rows, same, ahead, behind, far):
     at_z = place_on_z()
-    blocks = [(offset, quad, block, quad) for offset, block in ((0, same), (1, ahead), (15, behind)) for quad in range(4)]
-    blocks += [(2, 0, far_a, 0), (2, 1, far_a, 1), (14, 3, far_b, 0), (14, 0, far_b, 1)]
-    for offset, quad, block, slot in blocks:
-        start = lax.rem(at_z + offset + 4 * quad, 16)
-        for which in range(2):
-            rows[which, pl.ds(pl.multiple_of(64 * start, 64), 64)] = block[slot, which]
+    for offset, block in ((0, same), (1, ahead), (2, far), (15, behind)):
+        for quad in range(4):
+            start = lax.rem(at_z + offset + 4 * quad, 16)
+            for which in range(2):
+                rows[which, pl.ds(pl.multiple_of(64 * start, 64), 64)] = block[quad, which]
 
 
 def lay_weights(weights, block, at_core):
@@ -123,13 +122,14 @@
                 weights[1, part, 128 * q : 128 * q + 128] = block[x, start : start + 64]
 
 
-def own_kernel(same, ahead, behind, far_a, far_b, blocks, rows, weights):
-    lay_rows(rows, same, ahead, behind, far_a, far_b)
-    lay_weights(weights, blocks, lax.axis_index("core"))
-
-
-def first_kernel(rows, begun, core_blocks, weights, terms):
-    lay_weights(weights, core_blocks, 1 - lax.axis_index("core"))
+def rows_kernel(same, ahead, behind, far, _, rows):
+    lay_rows(rows, same, ahead, behind, far)
+
+
+def first_kernel(rows, blocks, core_blocks, weights, terms):
+    core = lax.axis_index("core")
+    lay_weights(weights, blocks, core)
+    lay_weights(weights, core_blocks, 1 - core)
     for which in range(2):
         product = lax.dot_general(
             rows[which], weights[which], (((0,), (0,)), ((), ())), preferred_element_type=F32
@@ -169,14 +169,13 @@
                 out[slot, which] = rows[which, pl.ds(pl.multiple_of(256 * group + 64 * at, 64), 64)]
 
 
-def call(kernel, shapes, *operands, scratch=(), space=VMEM, out_space=VMEM, mib=20, aliases={}, cost=None):
+def call(kernel, shapes, *operands, scratch=(), space=VMEM, out_space=VMEM, mib=20, cost=None):
     return pl.pallas_call(
         kernel,
         out_shape=[jax.ShapeDtypeStruct(shape, BF16) for shape in shapes],
         in_specs=[space] * len(operands),
         out_specs=[out_space] * len(shapes),
         scratch_shapes=[pltpu.VMEM(shape, BF16) if isinstance(shape, tuple) else shape for shape in scratch],
-        input_output_aliases=aliases,
         cost_estimate=pl.CostEstimate(flops=cost, bytes_accessed=0, transcendentals=0) if cost else None,
         compiler_params=pltpu.CompilerParams(vmem_limit_bytes=mib * 2**20),
     )(*operands)
@@ -198,15 +197,10 @@
     blocks = exchange(blocks, "x")
     same = jnp.stack([own, next_rows, along_z(next_rows, -4), last_rows])
     behind, ahead = along_z(same, 1), along_z(same, -1)
-    far_a, far_b = along_z(same[:2], -2), along_z(jnp.stack([last_rows, own]), 2)
-    rows, begun = call(
-        own_kernel, [(2, 1024, 256), (2, 1024, 1024)], same, ahead, behind, far_a, far_b, blocks, cost=COST
-    )
+    far = along_z(same, -2)
+    (rows,) = call(rows_kernel, [(2, 1024, 256)], same, ahead, behind, far, blocks, cost=COST)
     weights, terms = call(
-        first_kernel,
-        [(2, 1024, 1024), (4, 2, 256, 256)],
-        rows, begun, swap(blocks, "core"),
-        aliases={1: 0},
+        first_kernel, [(2, 1024, 1024), (4, 2, 256, 256)], rows, blocks, swap(blocks, "core")
     )
     (hidden,) = call(middle_kernel, [(4, 2, 256, 256)], exchange(terms, "y"))
     hidden = exchange(hidden, "y")

time: 173 us -> 173 us (level); the launches traced: 172 us -> 170 us
  starting transfers between devices: 55.9 us -> 49.8 us
  waiting for transfers between devices: 48.9 us -> 53.5 us
    ppermute x11 -> x10, starting transfers between devices: 49 us -> 43 us  [along_z(): lax.ppermute(block, ALONG_Z, [(index(z), index((z + distance) % 16)) for...]
    all_to_all x1, waiting for transfers between devices: 0.01 us -> 4.84 us  [exchange(): return lax.all_to_all(parts, axis, split_axis=0, concat_axis=0, tiled=True)]
    ppermute x11 -> x10, waiting for transfers between devices: 48.9 us -> 48.6 us  [along_z(): lax.ppermute(block, ALONG_Z, [(index(z), index((z + distance) % 16)) for...]
  transfers between devices with their start and end apart: 13 -> 12, of which waited for: 6 -> 7; matrix products, arithmetic and copies ran while one was open for 0% -> 0% of each run, Pallas kernels for 0% -> 0%
where the time goes in v4:
time: 173 us; the launch traced here: 170 us
  blocking collectives  57.4 us (33%)
  waiting for transfers between devices  53.5 us (31%)
  starting transfers between devices  49.8 us (29%)
  Pallas kernels  6.48 us (4%)
  local copies, waits for them, and re-layouts  1.97 us (1%)
    all_to_all x3, blocking collectives, exchange(): return lax.all_to_all(parts, axis, split_axis=0, concat_axis=0, tiled=True)  57.4 us
    ppermute x10, waiting for transfers between devices, along_z(): lax.ppermute(block, ALONG_Z, [(index(z), index((z + distance) % 16)) for...  48.6 us
    ppermute x10, starting transfers between devices, along_z(): lax.ppermute(block, ALONG_Z, [(index(z), index((z + distance) % 16)) for...  43 us
    pallas_call x6, Pallas kernels, call(): pl.pallas_call(kernel, out_shape=[jax.ShapeDtypeStruct(shape, BF16) for s...  6.48 us
    all_to_all x1, starting transfers between devices, exchange(): return lax.all_to_all(parts, axis, split_axis=0, concat_axis=0, tiled=True)  4.9 us
    all_to_all x1, waiting for transfers between devices, exchange(): return lax.all_to_all(parts, axis, split_axis=0, concat_axis=0, tiled=True)  4.84 us
  transfers between devices with their start and end apart: 12, of which 7 were waited for; matrix products, arithmetic and copies ran while one was open for 0% of the time, Pallas kernels for 0%

profile of v4, /device:TPU:6, one launch (start us, length us, event | category | flops | bytes accessed | tf_op | source)
XLA Modules:
  0.0 170.2 jit_solution(9092415181268645094)
XLA Ops:
  0.6 2.1 %shard_map.68 = (bf16[2,64,256]{2,1,0:T(8,128)(2,1)}, bf16[1280,128]{1,0:T(8,128)(2,1)}, bf16[1280,128]{1,0:T(8,128)(2,1)}) custom-call(bf16[64,256]{1,0:T(8,128)(2,1)} %bitcast.21, bf16[64,256]{1,0:T(8,128)(2,1)} %bitcast.22, s32[1,256]{1,0:T(1,128)} %bitcast.23, bf16[512,256]{1,0:T(8,128)(2,1)} %refs_3_.1, bf16[64,2048]{1,0:T(8,128)(2,1)} %bitcast.18), custom_call_target="tpu_custom_call" | custom-call | tf_op jit(solution)/shard_map/pallas_call | solution.py:173
  2.8 9.1 %collective-permute-start = (bf16[1280,128]{1,0:T(8,128)(2,1)}, bf16[1280,128]{1,0:T(8,128)(2,1)S(1)}, u32[]{:S(2)}, u32[]{:S(2)}) collective-permute-start(bf16[1280,128]{1,0:T(8,128)(2,1)} %get-tuple-element.16), channel_id=1, source_target_pairs={{0,32},{8,40},{16,48},{24,56},{32,4},{40,12},{48,20},{56,28},{4,36... | collective-permute-start | bytes 983048 | tf_op jit(solution)/shard_map/ppermute | solution.py:35
  11.9 5.6 %collective-permute-start.1 = (bf16[1280,128]{1,0:T(8,128)(2,1)}, bf16[1280,128]{1,0:T(8,128)(2,1)S(1)}, u32[]{:S(2)}, u32[]{:S(2)}) collective-permute-start(bf16[1280,128]{1,0:T(8,128)(2,1)} %get-tuple-element.17), channel_id=1, source_target_pairs={{0,36},{8,44},{16,52},{24,60},{32,0},{40,8},{48,16},{56,24},{4,32}... | collective-permute-start | bytes 983048 | tf_op jit(solution)/shard_map/ppermute | solution.py:35
  17.4 10.7 %collective-permute-done.below = bf16[1280,128]{1,0:T(8,128)(2,1)S(1)} collective-permute-done((bf16[1280,128]{1,0:T(8,128)(2,1)}, bf16[1280,128]{1,0:T(8,128)(2,1)S(1)}, u32[]{:S(2)}, u32[]{:S(2)}) %collective-permute-start) | collective-permute-done | bytes 327712 | tf_op jit(solution)/shard_map/ppermute | solution.py:35
  28.1 21.7 %collective-permute-done.1.above = bf16[1280,128]{1,0:T(8,128)(2,1)S(1)} collective-permute-done((bf16[1280,128]{1,0:T(8,128)(2,1)}, bf16[1280,128]{1,0:T(8,128)(2,1)S(1)}, u32[]{:S(2)}, u32[]{:S(2)}) %collective-permute-start.1) | collective-permute-done | bytes 327712 | tf_op jit(solution)/shard_map/ppermute | solution.py:35
  49.8 0.3 shard_map.69
  50.1 0.0 copy-start
  50.1 1.3 copy-done
  51.5 0.0 copy-start.1
  51.5 4.9 %all-to-all-start = ((bf16[4,2048,128]{2,1,0:T(8,128)(2,1)}), bf16[4,2048,128]{2,1,0:T(8,128)(2,1)S(1)}, u32[]{:S(2)}, u32[]{:S(2)}) async-start(bf16[4,2048,128]{2,1,0:T(8,128)(2,1)} %copy-done), calls=%async_computation | async-start | bytes 4194304 | tf_op jit(solution)/shard_map/all_to_all | solution.py:22
  56.4 4.4 %collective-permute-start.2 = (bf16[2,64,256]{2,1,0:T(8,128)(2,1)S(1)}, bf16[2,64,256]{2,1,0:T(8,128)(2,1)S(1)}, u32[]{:S(2)}, u32[]{:S(2)}) collective-permute-start(bf16[2,64,256]{2,1,0:T(8,128)(2,1)S(1)} %get-tuple-element.18), channel_id=1, source_target_pairs={{0,36},{8,44},{16,52},{24,60},{32,0},{40,8},{48,16},{56,24},{4,32}... | collective-permute-start | bytes 196616 | tf_op jit(solution)/shard_map/ppermute | solution.py:35
  60.8 5.7 %collective-permute-done.2 = bf16[2,64,256]{2,1,0:T(8,128)(2,1)S(1)} collective-permute-done((bf16[2,64,256]{2,1,0:T(8,128)(2,1)S(1)}, bf16[2,64,256]{2,1,0:T(8,128)(2,1)S(1)}, u32[]{:S(2)}, u32[]{:S(2)}) %collective-permute-start.2) | collective-permute-done | bytes 65568 | tf_op jit(solution)/shard_map/ppermute | solution.py:35
  66.4 0.0 copy-done.1
  66.5 1.9 %collective-permute-start.5 = (bf16[4,2,64,256]{3,2,1,0:T(8,128)(2,1)S(1)}, bf16[4,2,64,256]{3,2,1,0:T(8,128)(2,1)S(1)}, u32[]{:S(2)}, u32[]{:S(2)}) collective-permute-start(bf16[4,2,64,256]{3,2,1,0:T(8,128)(2,1)S(1)} %pad_maximum_fusion.same), channel_id=1, source_target_pairs={{0,52},{8,60},{16,0},{24,8},{32,16},{40,24},{48,32},{56,40},{4,48}... | collective-permute-start | bytes 786440 | tf_op jit(solution)/shard_map/ppermute | solution.py:35
  68.4 3.3 %collective-permute-start.4 = (bf16[4,2,64,256]{3,2,1,0:T(8,128)(2,1)S(1)}, bf16[4,2,64,256]{3,2,1,0:T(8,128)(2,1)S(1)}, u32[]{:S(2)}, u32[]{:S(2)}) collective-permute-start(bf16[4,2,64,256]{3,2,1,0:T(8,128)(2,1)S(1)} %pad_maximum_fusion.same), channel_id=1, source_target_pairs={{0,8},{8,16},{16,24},{24,32},{32,40},{40,48},{48,56},{56,4},{4,12}... | collective-permute-start | bytes 786440 | tf_op jit(solution)/shard_map/ppermute | solution.py:35
  71.7 3.8 %collective-permute-start.3 = (bf16[4,2,64,256]{3,2,1,0:T(8,128)(2,1)S(1)}, bf16[4,2,64,256]{3,2,1,0:T(8,128)(2,1)S(1)}, u32[]{:S(2)}, u32[]{:S(2)}) collective-permute-start(bf16[4,2,64,256]{3,2,1,0:T(8,128)(2,1)S(1)} %pad_maximum_fusion.same), channel_id=1, source_target_pairs={{0,60},{8,0},{16,8},{24,16},{32,24},{40,32},{48,40},{56,48},{4,56}... | collective-permute-start | bytes 786440 | tf_op jit(solution)/shard_map/ppermute | solution.py:35
  75.5 4.8 %all-to-all-done._.blocks = bf16[4,2048,128]{2,1,0:T(8,128)(2,1)S(1)} async-done(((bf16[4,2048,128]{2,1,0:T(8,128)(2,1)}), bf16[4,2048,128]{2,1,0:T(8,128)(2,1)S(1)}, u32[]{:S(2)}, u32[]{:S(2)}) %all-to-all-start) | async-done | bytes 2097184 | tf_op jit(solution)/shard_map/all_to_all | solution.py:22
  80.3 1.9 %collective-permute-start.6 = (bf16[4,2048,128]{2,1,0:T(8,128)(2,1)S(1)}, bf16[4,2048,128]{2,1,0:T(8,128)(2,1)S(1)}, u32[]{:S(2)}, u32[]{:S(2)}) collective-permute-start(bf16[4,2048,128]{2,1,0:T(8,128)(2,1)S(1)} %all-to-all-done._.blocks), channel_id=1, source_target_pairs={{0,64},{64,0},{1,65},{65,1},{2,66},{66,2},{3,67},{67,3},{4,68},{68... | collective-permute-start | bytes 6291464 | tf_op jit(solution)/shard_map/ppermute | solution.py:30
  82.2 0.0 collective-permute-done.5.far
  82.2 0.0 collective-permute-done.4.behind
  82.2 4.3 %collective-permute-done.3.ahead = bf16[4,2,64,256]{3,2,1,0:T(8,128)(2,1)S(1)} collective-permute-done((bf16[4,2,64,256]{3,2,1,0:T(8,128)(2,1)S(1)}, bf16[4,2,64,256]{3,2,1,0:T(8,128)(2,1)S(1)}, u32[]{:S(2)}, u32[]{:S(2)}) %collective-permute-start.3) | collective-permute-done | bytes 262176 | tf_op jit(solution)/shard_map/ppermute | solution.py:35
  86.6 0.1 shard_map.70.rows
  86.7 0.0 collective-permute-done.6.core_blocks
  86.7 2.3 %shard_map.71 = (bf16[2,1024,1024]{2,1,0:T(8,128)(2,1)S(1)}, bf16[4,2,256,256]{3,2,1,0:T(8,128)(2,1)S(1)}) custom-call(bf16[2,1024,256]{2,1,0:T(8,128)(2,1)S(1)} %shard_map.70.rows, bf16[4,2048,128]{2,1,0:T(8,128)(2,1)S(1)} %all-to-all-done._.blocks, bf16[4,2048,128]{2,1,0:T(8,128)(2,1)S(1)} %collective-permute-done.6.core_blocks), custom_call_target="tpu_custom_call" | custom-call | tf_op jit(solution)/shard_map/pallas_call | solution.py:173
  89.0 19.3 %all_to_all.20.terms = bf16[4,2,256,256]{3,2,1,0:T(8,128)(2,1)S(1)} all-to-all(bf16[4,2,256,256]{3,2,1,0:T(8,128)(2,1)S(1)} %get-tuple-element.21), channel_id=1, replica_groups=mesh['x'=4,'core'=2,'quad'=2,'place'=4,'half'=2,'y'=4] {'y'}, dimensions={0} | all-to-all | bytes 2097152 | tf_op jit(solution)/shard_map/all_to_all | solution.py:22
  108.3 0.3 shard_map.72
  108.6 16.6 %all_to_all.21.hidden = bf16[4,2,256,256]{3,2,1,0:T(8,128)(2,1)S(1)} all-to-all(bf16[4,2,256,256]{3,2,1,0:T(8,128)(2,1)S(1)} %shard_map.72), channel_id=1, replica_groups=mesh['x'=4,'core'=2,'quad'=2,'place'=4,'half'=2,'y'=4] {'y'}, dimensions={0} | all-to-all | bytes 2097152 | tf_op jit(solution)/shard_map/all_to_all | solution.py:22
  125.2 1.3 shard_map.73
  126.5 1.9 %collective-permute-start.7 = (bf16[4,2,64,256]{3,2,1,0:T(8,128)(2,1)S(1)}, bf16[4,2,64,256]{3,2,1,0:T(8,128)(2,1)S(1)}, u32[]{:S(2)}, u32[]{:S(2)}) collective-permute-start(bf16[4,2,64,256]{3,2,1,0:T(8,128)(2,1)S(1)} %get-tuple-element.24), channel_id=1, source_target_pairs={{0,8},{8,16},{16,24},{24,32},{32,40},{40,48},{48,56},{56,4},{4,12}... | collective-permute-start | bytes 786440 | tf_op jit(solution)/shard_map/ppermute | solution.py:35
  128.4 5.1 %collective-permute-start.8 = (bf16[4,2,64,256]{3,2,1,0:T(8,128)(2,1)S(1)}, bf16[4,2,64,256]{3,2,1,0:T(8,128)(2,1)S(1)}, u32[]{:S(2)}, u32[]{:S(2)}) collective-permute-start(bf16[4,2,64,256]{3,2,1,0:T(8,128)(2,1)S(1)} %get-tuple-element.25), channel_id=1, source_target_pairs={{0,60},{8,0},{16,8},{24,16},{32,24},{40,32},{48,40},{56,48},{4,56}... | collective-permute-start | bytes 786440 | tf_op jit(solution)/shard_map/ppermute | solution.py:35
  133.6 1.9 %collective-permute-start.9 = (bf16[2,2,64,256]{3,2,1,0:T(8,128)(2,1)S(1)}, bf16[2,2,64,256]{3,2,1,0:T(8,128)(2,1)S(1)}, u32[]{:S(2)}, u32[]{:S(2)}) collective-permute-start(bf16[2,2,64,256]{3,2,1,0:T(8,128)(2,1)S(1)} %get-tuple-element.26), channel_id=1, source_target_pairs={{0,16},{8,24},{16,32},{24,40},{32,48},{40,56},{48,4},{56,12},{4,20... | collective-permute-start | bytes 393224 | tf_op jit(solution)/shard_map/ppermute | solution.py:35
  135.5 6.0 %collective-permute-start.10 = (bf16[2,2,64,256]{3,2,1,0:T(8,128)(2,1)S(1)}, bf16[2,2,64,256]{3,2,1,0:T(8,128)(2,1)S(1)}, u32[]{:S(2)}, u32[]{:S(2)}) collective-permute-start(bf16[2,2,64,256]{3,2,1,0:T(8,128)(2,1)S(1)} %get-tuple-element.27), channel_id=1, source_target_pairs={{0,52},{8,60},{16,0},{24,8},{32,16},{40,24},{48,32},{56,40},{4,48}... | collective-permute-start | bytes 393224 | tf_op jit(solution)/shard_map/ppermute | solution.py:35
  141.6 2.1 %collective-permute-done.9 = bf16[2,2,64,256]{3,2,1,0:T(8,128)(2,1)S(1)} collective-permute-done((bf16[2,2,64,256]{3,2,1,0:T(8,128)(2,1)S(1)}, bf16[2,2,64,256]{3,2,1,0:T(8,128)(2,1)S(1)}, u32[]{:S(2)}, u32[]{:S(2)}) %collective-permute-start.9) | collective-permute-done | bytes 131104 | tf_op jit(solution)/shard_map/ppermute | solution.py:35
  143.6 4.2 %collective-permute-done.10 = bf16[2,2,64,256]{3,2,1,0:T(8,128)(2,1)S(1)} collective-permute-done((bf16[2,2,64,256]{3,2,1,0:T(8,128)(2,1)S(1)}, bf16[2,2,64,256]{3,2,1,0:T(8,128)(2,1)S(1)}, u32[]{:S(2)}, u32[]{:S(2)}) %collective-permute-start.10) | collective-permute-done | bytes 131104 | tf_op jit(solution)/shard_map/ppermute | solution.py:35
  147.8 0.0 collective-permute-done.7
  147.9 0.0 collective-permute-done.8
  147.9 0.1 add_convert_fusion
  148.0 21.5 %all_to_all.22 = bf16[4,2,64,256]{3,2,1,0:T(8,128)(2,1)S(1)} all-to-all(bf16[4,2,64,256]{3,2,1,0:T(8,128)(2,1)S(1)} %add_convert_fusion), channel_id=1, replica_groups=mesh['x'=4,'core'=2,'quad'=2,'place'=4,'half'=2,'y'=4] {'half','quad'}, dimensions={0} | all-to-all | bytes 524288 | tf_op jit(solution)/shard_map/all_to_all | solution.py:22
  169.6 0.6 slice_bitcast_fusion
  (3 shorter events, 0.1 us)
Async XLA Ops:
  2.8 25.4 %collective-permute-start = (bf16[1280,128]{1,0:T(8,128)(2,1)}, bf16[1280,128]{1,0:T(8,128)(2,1)S(1)}, u32[]{:S(2)}, u32[]{:S(2)}) collective-permute-start(bf16[1280,128]{1,0:T(8,128)(2,1)} %get-tuple-element.16), channel_id=1, source_target_pairs={{0,32},{8,40},{16,48},{24,56},{32,4},{40,12},{48,20},{56,28},{4,36... | collective-permute-start | bytes 983048 | tf_op jit(solution)/shard_map/ppermute | solution.py:35
  11.9 37.9 %collective-permute-start.1 = (bf16[1280,128]{1,0:T(8,128)(2,1)}, bf16[1280,128]{1,0:T(8,128)(2,1)S(1)}, u32[]{:S(2)}, u32[]{:S(2)}) collective-permute-start(bf16[1280,128]{1,0:T(8,128)(2,1)} %get-tuple-element.17), channel_id=1, source_target_pairs={{0,36},{8,44},{16,52},{24,60},{32,0},{40,8},{48,16},{56,24},{4,32}... | collective-permute-start | bytes 983048 | tf_op jit(solution)/shard_map/ppermute | solution.py:35
  50.1 1.3 copy-start
  51.5 15.0 %copy-start.1 = (bf16[2,64,256]{2,1,0:T(8,128)(2,1)S(1)}, bf16[2,64,256]{2,1,0:T(8,128)(2,1)}, u32[]{:S(2)}) copy-start(bf16[2,64,256]{2,1,0:T(8,128)(2,1)} %get-tuple-element.15) | copy-start | bytes 196612
  51.5 28.8 %all-to-all-start = ((bf16[4,2048,128]{2,1,0:T(8,128)(2,1)}), bf16[4,2048,128]{2,1,0:T(8,128)(2,1)S(1)}, u32[]{:S(2)}, u32[]{:S(2)}) async-start(bf16[4,2048,128]{2,1,0:T(8,128)(2,1)} %copy-done), calls=%async_computation | async-start | bytes 4194304 | tf_op jit(solution)/shard_map/all_to_all | solution.py:22
  56.4 10.1 %collective-permute-start.2 = (bf16[2,64,256]{2,1,0:T(8,128)(2,1)S(1)}, bf16[2,64,256]{2,1,0:T(8,128)(2,1)S(1)}, u32[]{:S(2)}, u32[]{:S(2)}) collective-permute-start(bf16[2,64,256]{2,1,0:T(8,128)(2,1)S(1)} %get-tuple-element.18), channel_id=1, source_target_pairs={{0,36},{8,44},{16,52},{24,60},{32,0},{40,8},{48,16},{56,24},{4,32}... | collective-permute-start | bytes 196616 | tf_op jit(solution)/shard_map/ppermute | solution.py:35
  66.5 15.8 %collective-permute-start.5 = (bf16[4,2,64,256]{3,2,1,0:T(8,128)(2,1)S(1)}, bf16[4,2,64,256]{3,2,1,0:T(8,128)(2,1)S(1)}, u32[]{:S(2)}, u32[]{:S(2)}) collective-permute-start(bf16[4,2,64,256]{3,2,1,0:T(8,128)(2,1)S(1)} %pad_maximum_fusion.same), channel_id=1, source_target_pairs={{0,52},{8,60},{16,0},{24,8},{32,16},{40,24},{48,32},{56,40},{4,48}... | collective-permute-start | bytes 786440 | tf_op jit(solution)/shard_map/ppermute | solution.py:35
  68.4 13.8 %collective-permute-start.4 = (bf16[4,2,64,256]{3,2,1,0:T(8,128)(2,1)S(1)}, bf16[4,2,64,256]{3,2,1,0:T(8,128)(2,1)S(1)}, u32[]{:S(2)}, u32[]{:S(2)}) collective-permute-start(bf16[4,2,64,256]{3,2,1,0:T(8,128)(2,1)S(1)} %pad_maximum_fusion.same), channel_id=1, source_target_pairs={{0,8},{8,16},{16,24},{24,32},{32,40},{40,48},{48,56},{56,4},{4,12}... | collective-permute-start | bytes 786440 | tf_op jit(solution)/shard_map/ppermute | solution.py:35
  71.7 14.9 %collective-permute-start.3 = (bf16[4,2,64,256]{3,2,1,0:T(8,128)(2,1)S(1)}, bf16[4,2,64,256]{3,2,1,0:T(8,128)(2,1)S(1)}, u32[]{:S(2)}, u32[]{:S(2)}) collective-permute-start(bf16[4,2,64,256]{3,2,1,0:T(8,128)(2,1)S(1)} %pad_maximum_fusion.same), channel_id=1, source_target_pairs={{0,60},{8,0},{16,8},{24,16},{32,24},{40,32},{48,40},{56,48},{4,56}... | collective-permute-start | bytes 786440 | tf_op jit(solution)/shard_map/ppermute | solution.py:35
  80.3 6.4 %collective-permute-start.6 = (bf16[4,2048,128]{2,1,0:T(8,128)(2,1)S(1)}, bf16[4,2048,128]{2,1,0:T(8,128)(2,1)S(1)}, u32[]{:S(2)}, u32[]{:S(2)}) collective-permute-start(bf16[4,2048,128]{2,1,0:T(8,128)(2,1)S(1)} %all-to-all-done._.blocks), channel_id=1, source_target_pairs={{0,64},{64,0},{1,65},{65,1},{2,66},{66,2},{3,67},{67,3},{4,68},{68... | collective-permute-start | bytes 6291464 | tf_op jit(solution)/shard_map/ppermute | solution.py:30
  126.5 21.3 %collective-permute-start.7 = (bf16[4,2,64,256]{3,2,1,0:T(8,128)(2,1)S(1)}, bf16[4,2,64,256]{3,2,1,0:T(8,128)(2,1)S(1)}, u32[]{:S(2)}, u32[]{:S(2)}) collective-permute-start(bf16[4,2,64,256]{3,2,1,0:T(8,128)(2,1)S(1)} %get-tuple-element.24), channel_id=1, source_target_pairs={{0,8},{8,16},{16,24},{24,32},{32,40},{40,48},{48,56},{56,4},{4,12}... | collective-permute-start | bytes 786440 | tf_op jit(solution)/shard_map/ppermute | solution.py:35
  128.4 19.4 %collective-permute-start.8 = (bf16[4,2,64,256]{3,2,1,0:T(8,128)(2,1)S(1)}, bf16[4,2,64,256]{3,2,1,0:T(8,128)(2,1)S(1)}, u32[]{:S(2)}, u32[]{:S(2)}) collective-permute-start(bf16[4,2,64,256]{3,2,1,0:T(8,128)(2,1)S(1)} %get-tuple-element.25), channel_id=1, source_target_pairs={{0,60},{8,0},{16,8},{24,16},{32,24},{40,32},{48,40},{56,48},{4,56}... | collective-permute-start | bytes 786440 | tf_op jit(solution)/shard_map/ppermute | solution.py:35
  133.6 10.0 %collective-permute-start.9 = (bf16[2,2,64,256]{3,2,1,0:T(8,128)(2,1)S(1)}, bf16[2,2,64,256]{3,2,1,0:T(8,128)(2,1)S(1)}, u32[]{:S(2)}, u32[]{:S(2)}) collective-permute-start(bf16[2,2,64,256]{3,2,1,0:T(8,128)(2,1)S(1)} %get-tuple-element.26), channel_id=1, source_target_pairs={{0,16},{8,24},{16,32},{24,40},{32,48},{40,56},{48,4},{56,12},{4,20... | collective-permute-start | bytes 393224 | tf_op jit(solution)/shard_map/ppermute | solution.py:35
  135.5 12.3 %collective-permute-start.10 = (bf16[2,2,64,256]{3,2,1,0:T(8,128)(2,1)S(1)}, bf16[2,2,64,256]{3,2,1,0:T(8,128)(2,1)S(1)}, u32[]{:S(2)}, u32[]{:S(2)}) collective-permute-start(bf16[2,2,64,256]{3,2,1,0:T(8,128)(2,1)S(1)} %get-tuple-element.27), channel_id=1, source_target_pairs={{0,52},{8,60},{16,0},{24,8},{32,16},{40,24},{48,32},{56,40},{4,48}... | collective-permute-start | bytes 393224 | tf_op jit(solution)/shard_map/ppermute | solution.py:35

commit v5 on v4

--- a/solution.py
+++ b/solution.py
@@ -110,32 +110,48 @@
                 rows[which, pl.ds(pl.multiple_of(64 * start, 64), 64)] = block[quad, which]
 
 
-def lay_weights(weights, block, at_core):
+def lay_share(block, ins, outs):
     half = lax.div(lax.rem(place_on_z() + 12, 16), 8)
     for at, at_half in ((0, half), (1024, 1 - half)):
         for x in range(4):
-            lanes = pl.ds(pl.multiple_of(256 * x + 128 * at_core, 128), 128)
-            weights[0, pl.ds(pl.multiple_of(512 * at_half, 512), 512), lanes] = block[x, at : at + 512]
-            part = pl.ds(pl.multiple_of(512 * at_half + 128 * x + 64 * at_core, 64), 64)
+            ins[pl.ds(pl.multiple_of(512 * at_half, 512), 512), 128 * x : 128 * x + 128] = block[x, at : at + 512]
+            part = pl.ds(pl.multiple_of(256 * at_half + 64 * x, 64), 64)
             for q in range(8):
                 start = at + 512 + 64 * q
-                weights[1, part, 128 * q : 128 * q + 128] = block[x, start : start + 64]
-
-
-def rows_kernel(same, ahead, behind, far, _, rows):
+                outs[part, 128 * q : 128 * q + 128] = block[x, start : start + 64]
+
+
+def share_of(core):
+    return [pl.multiple_of(512 * half + 128 * x + 64 * core, 64) for half in range(2) for x in range(4)]
+
+
+def share_products(rows, ins, outs, core):
+    masked = jnp.concatenate([rows[1, pl.ds(start, 64)] for start in share_of(core)], axis=0)
+    contract = (((0,), (0,)), ((), ()))
+    return (
+        lax.dot_general(rows[0], ins[...], contract, preferred_element_type=F32),
+        lax.dot_general(masked, outs[...], contract, preferred_element_type=F32),
+    )
+
+
+def own_kernel(same, ahead, behind, far, block, rows, ins, outs, preact, grad):
     lay_rows(rows, same, ahead, behind, far)
-
-
-def first_kernel(rows, blocks, core_blocks, weights, terms):
+    lay_share(block, ins, outs)
+    own_preact, own_grad = share_products(rows, ins, outs, lax.axis_index("core"))
+    preact[...] = own_preact.astype(BF16)
+    grad[...] = own_grad
+
+
+def first_kernel(rows, block, preact, grad, ins, outs, terms):
     core = lax.axis_index("core")
-    lay_weights(weights, blocks, core)
-    lay_weights(weights, core_blocks, 1 - core)
-    for which in range(2):
-        product = lax.dot_general(
-            rows[which], weights[which], (((0,), (0,)), ((), ())), preferred_element_type=F32
-        )
-        for part in range(4):
-            terms[part, which] = product[:, 256 * part : 256 * part + 256].astype(BF16)
+    lay_share(block, ins, outs)
+    other_preact, other_grad = share_products(rows, ins, outs, 1 - core)
+    other_preact = other_preact.astype(BF16)
+    total = (grad[...] + other_grad).astype(BF16)
+    for x in range(4):
+        terms[x, 0, :, pl.ds(pl.multiple_of(128 * core, 128), 128)] = preact[:, 128 * x : 128 * x + 128]
+        terms[x, 0, :, pl.ds(pl.multiple_of(128 * (1 - core), 128), 128)] = other_preact[:, 128 * x : 128 * x + 128]
+        terms[x, 1] = total[:, 256 * x : 256 * x + 256]
 
 
 def middle_kernel(terms, hidden):
@@ -149,14 +165,19 @@
         hidden[part, 1] = grad
 
 
-def second_kernel(hidden, weights, same, ahead, behind, far_a, far_b, rows):
-    place = lax.axis_index("place")
-    for which in range(2):
-        block = jnp.concatenate([hidden[part, which] for part in range(4)], axis=1)
-        product = lax.dot_general(
-            weights[1 - which], block, (((1,), (1,)), ((), ())), preferred_element_type=F32
-        )
-        rows[which] = product.astype(BF16)
+def second_kernel(hidden, own_ins, own_outs, other_ins, other_outs, same, ahead, behind, far_a, far_b, rows):
+    core, place = lax.axis_index("core"), lax.axis_index("place")
+    contract = (((1,), (1,)), ((), ()))
+    block = jnp.concatenate([hidden[x, 0] for x in range(4)], axis=1)
+    grad = jnp.zeros((1024, 256), F32)
+    for at_core, ins, outs in ((core, own_ins, own_outs), (1 - core, other_ins, other_outs)):
+        product = lax.dot_general(outs[...], block, contract, preferred_element_type=F32).astype(BF16)
+        for i, start in enumerate(share_of(at_core)):
+            rows[0, pl.ds(start, 64)] = product[64 * i : 64 * i + 64]
+        lanes = pl.ds(pl.multiple_of(128 * at_core, 128), 128)
+        part = jnp.concatenate([hidden[x, 1, :, lanes] for x in range(4)], axis=1)
+        grad += lax.dot_general(ins[...], part, contract, preferred_element_type=F32)
+    rows[1] = grad.astype(BF16)
     for group in range(4):
         for which in range(2):
             for offset, out, slot in (
@@ -172,7 +193,7 @@
 def call(kernel, shapes, *operands, scratch=(), space=VMEM, out_space=VMEM, mib=20, cost=None):
     return pl.pallas_call(
         kernel,
-        out_shape=[jax.ShapeDtypeStruct(shape, BF16) for shape in shapes],
+        out_shape=[jax.ShapeDtypeStruct(shape, BF16) if isinstance(shape, tuple) else shape for shape in shapes],
         in_specs=[space] * len(operands),
         out_specs=[out_space] * len(shapes),
         scratch_shapes=[pltpu.VMEM(shape, BF16) if isinstance(shape, tuple) else shape for shape in scratch],
@@ -198,15 +219,22 @@
     same = jnp.stack([own, next_rows, along_z(next_rows, -4), last_rows])
     behind, ahead = along_z(same, 1), along_z(same, -1)
     far = along_z(same, -2)
-    (rows,) = call(rows_kernel, [(2, 1024, 256)], same, ahead, behind, far, blocks, cost=COST)
-    weights, terms = call(
-        first_kernel, [(2, 1024, 1024), (4, 2, 256, 256)], rows, blocks, swap(blocks, "core")
+    share = [(1024, 512), (512, 1024)]
+    rows, ins, outs, preact, grad = call(
+        own_kernel,
+        [(2, 1024, 256)] + share + [(256, 512), jax.ShapeDtypeStruct((256, 1024), F32)],
+        same, ahead, behind, far, blocks,
+        cost=COST,
+    )
+    other_ins, other_outs, terms = call(
+        first_kernel, share + [(4, 2, 256, 256)], rows, swap(blocks, "core"), preact, grad
     )
     (hidden,) = call(middle_kernel, [(4, 2, 256, 256)], exchange(terms, "y"))
     hidden = exchange(hidden, "y")
     whole, part = (4, 2, 64, 256), (2, 2, 64, 256)
     same, ahead, behind, far_a, far_b = call(
-        second_kernel, [whole, whole, whole, part, part], hidden, weights, scratch=[(2, 1024, 256)]
+        second_kernel, [whole, whole, whole, part, part], hidden, ins, outs, other_ins, other_outs,
+        scratch=[(2, 1024, 256)],
     )
     sums = [along_z(ahead, 1), along_z(behind, -1), jnp.concatenate([along_z(far_a, 2), along_z(far_b, -2)])]
     terms = same.astype(F32) + sum(block.astype(F32) for block in sums)

time: 173 us -> 172 us (level)
  transfers between devices with their start and end apart: 12 -> 12, of which waited for: 7 -> 7; matrix products, arithmetic and copies ran while one was open for 0% -> 0% of each run, Pallas kernels for 0% -> 1%
where the time goes in v5:
time: 172 us; the launch traced here: 169 us
  blocking collectives  56.6 us (33%)
  waiting for transfers between devices  53.3 us (31%)
  starting transfers between devices  49.8 us (29%)
  Pallas kernels  6.42 us (4%)
  local copies, waits for them, and re-layouts  1.96 us (1%)
    all_to_all x3, blocking collectives, exchange(): return lax.all_to_all(parts, axis, split_axis=0, concat_axis=0, tiled=True)  56.6 us
    ppermute x10, waiting for transfers between devices, along_z(): lax.ppermute(block, ALONG_Z, [(index(z), index((z + distance) % 16)) for...  48.5 us
    ppermute x10, starting transfers between devices, along_z(): lax.ppermute(block, ALONG_Z, [(index(z), index((z + distance) % 16)) for...  43 us
    pallas_call x6, Pallas kernels, call(): pl.pallas_call(kernel, out_shape=[jax.ShapeDtypeStruct(shape, BF16) if is...  6.42 us
    all_to_all x1, starting transfers between devices, exchange(): return lax.all_to_all(parts, axis, split_axis=0, concat_axis=0, tiled=True)  4.9 us
    all_to_all x1, waiting for transfers between devices, exchange(): return lax.all_to_all(parts, axis, split_axis=0, concat_axis=0, tiled=True)  4.84 us
  transfers between devices with their start and end apart: 12, of which 7 were waited for; matrix products, arithmetic and copies ran while one was open for 0% of the time, Pallas kernels for 1%

profile of v5, /device:TPU:6, one launch (start us, length us, event | category | flops | bytes accessed | tf_op | source)
XLA Modules:
  0.0 169.1 jit_solution(11829804631912077463)
XLA Ops:
  0.6 2.1 %shard_map.68 = (bf16[2,64,256]{2,1,0:T(8,128)(2,1)}, bf16[1280,128]{1,0:T(8,128)(2,1)}, bf16[1280,128]{1,0:T(8,128)(2,1)}) custom-call(bf16[64,256]{1,0:T(8,128)(2,1)} %bitcast.21, bf16[64,256]{1,0:T(8,128)(2,1)} %bitcast.22, s32[1,256]{1,0:T(1,128)} %bitcast.23, bf16[512,256]{1,0:T(8,128)(2,1)} %refs_3_.1, bf16[64,2048]{1,0:T(8,128)(2,1)} %bitcast.18), custom_call_target="tpu_custom_call" | custom-call | tf_op jit(solution)/shard_map/pallas_call | solution.py:194
  2.7 9.1 %collective-permute-start = (bf16[1280,128]{1,0:T(8,128)(2,1)}, bf16[1280,128]{1,0:T(8,128)(2,1)S(1)}, u32[]{:S(2)}, u32[]{:S(2)}) collective-permute-start(bf16[1280,128]{1,0:T(8,128)(2,1)} %get-tuple-element.22), channel_id=1, source_target_pairs={{0,32},{8,40},{16,48},{24,56},{32,4},{40,12},{48,20},{56,28},{4,36... | collective-permute-start | bytes 983048 | tf_op jit(solution)/shard_map/ppermute | solution.py:35
  11.8 5.6 %collective-permute-start.1 = (bf16[1280,128]{1,0:T(8,128)(2,1)}, bf16[1280,128]{1,0:T(8,128)(2,1)S(1)}, u32[]{:S(2)}, u32[]{:S(2)}) collective-permute-start(bf16[1280,128]{1,0:T(8,128)(2,1)} %get-tuple-element.23), channel_id=1, source_target_pairs={{0,36},{8,44},{16,52},{24,60},{32,0},{40,8},{48,16},{56,24},{4,32}... | collective-permute-start | bytes 983048 | tf_op jit(solution)/shard_map/ppermute | solution.py:35
  17.4 10.7 %collective-permute-done.below = bf16[1280,128]{1,0:T(8,128)(2,1)S(1)} collective-permute-done((bf16[1280,128]{1,0:T(8,128)(2,1)}, bf16[1280,128]{1,0:T(8,128)(2,1)S(1)}, u32[]{:S(2)}, u32[]{:S(2)}) %collective-permute-start) | collective-permute-done | bytes 327712 | tf_op jit(solution)/shard_map/ppermute | solution.py:35
  28.1 21.7 %collective-permute-done.1.above = bf16[1280,128]{1,0:T(8,128)(2,1)S(1)} collective-permute-done((bf16[1280,128]{1,0:T(8,128)(2,1)}, bf16[1280,128]{1,0:T(8,128)(2,1)S(1)}, u32[]{:S(2)}, u32[]{:S(2)}) %collective-permute-start.1) | collective-permute-done | bytes 327712 | tf_op jit(solution)/shard_map/ppermute | solution.py:35
  49.8 0.3 shard_map.69
  50.1 0.0 copy-start
  50.1 1.3 copy-done
  51.5 0.0 copy-start.1
  51.5 4.9 %all-to-all-start = ((bf16[4,2048,128]{2,1,0:T(8,128)(2,1)}), bf16[4,2048,128]{2,1,0:T(8,128)(2,1)S(1)}, u32[]{:S(2)}, u32[]{:S(2)}) async-start(bf16[4,2048,128]{2,1,0:T(8,128)(2,1)} %copy-done), calls=%async_computation | async-start | bytes 4194304 | tf_op jit(solution)/shard_map/all_to_all | solution.py:22
  56.4 4.4 %collective-permute-start.2 = (bf16[2,64,256]{2,1,0:T(8,128)(2,1)S(1)}, bf16[2,64,256]{2,1,0:T(8,128)(2,1)S(1)}, u32[]{:S(2)}, u32[]{:S(2)}) collective-permute-start(bf16[2,64,256]{2,1,0:T(8,128)(2,1)S(1)} %get-tuple-element.24), channel_id=1, source_target_pairs={{0,36},{8,44},{16,52},{24,60},{32,0},{40,8},{48,16},{56,24},{4,32}... | collective-permute-start | bytes 196616 | tf_op jit(solution)/shard_map/ppermute | solution.py:35
  60.8 5.7 %collective-permute-done.2 = bf16[2,64,256]{2,1,0:T(8,128)(2,1)S(1)} collective-permute-done((bf16[2,64,256]{2,1,0:T(8,128)(2,1)S(1)}, bf16[2,64,256]{2,1,0:T(8,128)(2,1)S(1)}, u32[]{:S(2)}, u32[]{:S(2)}) %collective-permute-start.2) | collective-permute-done | bytes 65568 | tf_op jit(solution)/shard_map/ppermute | solution.py:35
  66.4 0.0 copy-done.1
  66.5 1.9 %collective-permute-start.5 = (bf16[4,2,64,256]{3,2,1,0:T(8,128)(2,1)S(1)}, bf16[4,2,64,256]{3,2,1,0:T(8,128)(2,1)S(1)}, u32[]{:S(2)}, u32[]{:S(2)}) collective-permute-start(bf16[4,2,64,256]{3,2,1,0:T(8,128)(2,1)S(1)} %pad_maximum_fusion.same), channel_id=1, source_target_pairs={{0,52},{8,60},{16,0},{24,8},{32,16},{40,24},{48,32},{56,40},{4,48}... | collective-permute-start | bytes 786440 | tf_op jit(solution)/shard_map/ppermute | solution.py:35
  68.4 3.3 %collective-permute-start.4 = (bf16[4,2,64,256]{3,2,1,0:T(8,128)(2,1)S(1)}, bf16[4,2,64,256]{3,2,1,0:T(8,128)(2,1)S(1)}, u32[]{:S(2)}, u32[]{:S(2)}) collective-permute-start(bf16[4,2,64,256]{3,2,1,0:T(8,128)(2,1)S(1)} %pad_maximum_fusion.same), channel_id=1, source_target_pairs={{0,8},{8,16},{16,24},{24,32},{32,40},{40,48},{48,56},{56,4},{4,12}... | collective-permute-start | bytes 786440 | tf_op jit(solution)/shard_map/ppermute | solution.py:35
  71.7 3.8 %collective-permute-start.3 = (bf16[4,2,64,256]{3,2,1,0:T(8,128)(2,1)S(1)}, bf16[4,2,64,256]{3,2,1,0:T(8,128)(2,1)S(1)}, u32[]{:S(2)}, u32[]{:S(2)}) collective-permute-start(bf16[4,2,64,256]{3,2,1,0:T(8,128)(2,1)S(1)} %pad_maximum_fusion.same), channel_id=1, source_target_pairs={{0,60},{8,0},{16,8},{24,16},{32,24},{40,32},{48,40},{56,48},{4,56}... | collective-permute-start | bytes 786440 | tf_op jit(solution)/shard_map/ppermute | solution.py:35
  75.5 4.8 %all-to-all-done.block = bf16[4,2048,128]{2,1,0:T(8,128)(2,1)S(1)} async-done(((bf16[4,2048,128]{2,1,0:T(8,128)(2,1)}), bf16[4,2048,128]{2,1,0:T(8,128)(2,1)S(1)}, u32[]{:S(2)}, u32[]{:S(2)}) %all-to-all-start) | async-done | bytes 2097184 | tf_op jit(solution)/shard_map/all_to_all | solution.py:22
  80.3 1.9 %collective-permute-start.6 = (bf16[4,2048,128]{2,1,0:T(8,128)(2,1)S(1)}, bf16[4,2048,128]{2,1,0:T(8,128)(2,1)S(1)}, u32[]{:S(2)}, u32[]{:S(2)}) collective-permute-start(bf16[4,2048,128]{2,1,0:T(8,128)(2,1)S(1)} %all-to-all-done.block), channel_id=1, source_target_pairs={{0,64},{64,0},{1,65},{65,1},{2,66},{66,2},{3,67},{67,3},{4,68},{68... | collective-permute-start | bytes 6291464 | tf_op jit(solution)/shard_map/ppermute | solution.py:30
  82.2 0.0 collective-permute-done.5.far
  82.2 0.0 collective-permute-done.4.behind
  82.2 4.3 %collective-permute-done.3.ahead = bf16[4,2,64,256]{3,2,1,0:T(8,128)(2,1)S(1)} collective-permute-done((bf16[4,2,64,256]{3,2,1,0:T(8,128)(2,1)S(1)}, bf16[4,2,64,256]{3,2,1,0:T(8,128)(2,1)S(1)}, u32[]{:S(2)}, u32[]{:S(2)}) %collective-permute-start.3) | collective-permute-done | bytes 262176 | tf_op jit(solution)/shard_map/ppermute | solution.py:35
  86.5 1.1 shard_map.70
  87.7 0.0 collective-permute-done.6.block
  87.7 1.1 shard_map.71
  88.8 19.1 %all_to_all.20.terms = bf16[4,2,256,256]{3,2,1,0:T(8,128)(2,1)S(1)} all-to-all(bf16[4,2,256,256]{3,2,1,0:T(8,128)(2,1)S(1)} %get-tuple-element.30), channel_id=1, replica_groups=mesh['x'=4,'core'=2,'quad'=2,'place'=4,'half'=2,'y'=4] {'y'}, dimensions={0} | all-to-all | bytes 2097152 | tf_op jit(solution)/shard_map/all_to_all | solution.py:22
  107.8 0.3 shard_map.72
  108.1 16.0 %all_to_all.21.hidden = bf16[4,2,256,256]{3,2,1,0:T(8,128)(2,1)S(1)} all-to-all(bf16[4,2,256,256]{3,2,1,0:T(8,128)(2,1)S(1)} %shard_map.72), channel_id=1, replica_groups=mesh['x'=4,'core'=2,'quad'=2,'place'=4,'half'=2,'y'=4] {'y'}, dimensions={0} | all-to-all | bytes 2097152 | tf_op jit(solution)/shard_map/all_to_all | solution.py:22
  124.2 1.5 shard_map.73
  125.6 1.9 %collective-permute-start.7 = (bf16[4,2,64,256]{3,2,1,0:T(8,128)(2,1)S(1)}, bf16[4,2,64,256]{3,2,1,0:T(8,128)(2,1)S(1)}, u32[]{:S(2)}, u32[]{:S(2)}) collective-permute-start(bf16[4,2,64,256]{3,2,1,0:T(8,128)(2,1)S(1)} %get-tuple-element.36), channel_id=1, source_target_pairs={{0,8},{8,16},{16,24},{24,32},{32,40},{40,48},{48,56},{56,4},{4,12}... | collective-permute-start | bytes 786440 | tf_op jit(solution)/shard_map/ppermute | solution.py:35
  127.6 5.1 %collective-permute-start.8 = (bf16[4,2,64,256]{3,2,1,0:T(8,128)(2,1)S(1)}, bf16[4,2,64,256]{3,2,1,0:T(8,128)(2,1)S(1)}, u32[]{:S(2)}, u32[]{:S(2)}) collective-permute-start(bf16[4,2,64,256]{3,2,1,0:T(8,128)(2,1)S(1)} %get-tuple-element.37), channel_id=1, source_target_pairs={{0,60},{8,0},{16,8},{24,16},{32,24},{40,32},{48,40},{56,48},{4,56}... | collective-permute-start | bytes 786440 | tf_op jit(solution)/shard_map/ppermute | solution.py:35
  132.7 1.9 %collective-permute-start.9 = (bf16[2,2,64,256]{3,2,1,0:T(8,128)(2,1)S(1)}, bf16[2,2,64,256]{3,2,1,0:T(8,128)(2,1)S(1)}, u32[]{:S(2)}, u32[]{:S(2)}) collective-permute-start(bf16[2,2,64,256]{3,2,1,0:T(8,128)(2,1)S(1)} %get-tuple-element.38), channel_id=1, source_target_pairs={{0,16},{8,24},{16,32},{24,40},{32,48},{40,56},{48,4},{56,12},{4,20... | collective-permute-start | bytes 393224 | tf_op jit(solution)/shard_map/ppermute | solution.py:35
  134.6 6.0 %collective-permute-start.10 = (bf16[2,2,64,256]{3,2,1,0:T(8,128)(2,1)S(1)}, bf16[2,2,64,256]{3,2,1,0:T(8,128)(2,1)S(1)}, u32[]{:S(2)}, u32[]{:S(2)}) collective-permute-start(bf16[2,2,64,256]{3,2,1,0:T(8,128)(2,1)S(1)} %get-tuple-element.39), channel_id=1, source_target_pairs={{0,52},{8,60},{16,0},{24,8},{32,16},{40,24},{48,32},{56,40},{4,48}... | collective-permute-start | bytes 393224 | tf_op jit(solution)/shard_map/ppermute | solution.py:35
  140.7 2.1 %collective-permute-done.9 = bf16[2,2,64,256]{3,2,1,0:T(8,128)(2,1)S(1)} collective-permute-done((bf16[2,2,64,256]{3,2,1,0:T(8,128)(2,1)S(1)}, bf16[2,2,64,256]{3,2,1,0:T(8,128)(2,1)S(1)}, u32[]{:S(2)}, u32[]{:S(2)}) %collective-permute-start.9) | collective-permute-done | bytes 131104 | tf_op jit(solution)/shard_map/ppermute | solution.py:35
  142.7 4.1 %collective-permute-done.10 = bf16[2,2,64,256]{3,2,1,0:T(8,128)(2,1)S(1)} collective-permute-done((bf16[2,2,64,256]{3,2,1,0:T(8,128)(2,1)S(1)}, bf16[2,2,64,256]{3,2,1,0:T(8,128)(2,1)S(1)}, u32[]{:S(2)}, u32[]{:S(2)}) %collective-permute-start.10) | collective-permute-done | bytes 131104 | tf_op jit(solution)/shard_map/ppermute | solution.py:35
  146.8 0.0 collective-permute-done.7
  146.8 0.0 collective-permute-done.8
  146.8 0.1 add_convert_fusion
  146.9 21.5 %all_to_all.22 = bf16[4,2,64,256]{3,2,1,0:T(8,128)(2,1)S(1)} all-to-all(bf16[4,2,64,256]{3,2,1,0:T(8,128)(2,1)S(1)} %add_convert_fusion), channel_id=1, replica_groups=mesh['x'=4,'core'=2,'quad'=2,'place'=4,'half'=2,'y'=4] {'half','quad'}, dimensions={0} | all-to-all | bytes 524288 | tf_op jit(solution)/shard_map/all_to_all | solution.py:22
  168.5 0.6 slice_bitcast_fusion
  (3 shorter events, 0.1 us)
Async XLA Ops:
  2.7 25.4 %collective-permute-start = (bf16[1280,128]{1,0:T(8,128)(2,1)}, bf16[1280,128]{1,0:T(8,128)(2,1)S(1)}, u32[]{:S(2)}, u32[]{:S(2)}) collective-permute-start(bf16[1280,128]{1,0:T(8,128)(2,1)} %get-tuple-element.22), channel_id=1, source_target_pairs={{0,32},{8,40},{16,48},{24,56},{32,4},{40,12},{48,20},{56,28},{4,36... | collective-permute-start | bytes 983048 | tf_op jit(solution)/shard_map/ppermute | solution.py:35
  11.8 37.9 %collective-permute-start.1 = (bf16[1280,128]{1,0:T(8,128)(2,1)}, bf16[1280,128]{1,0:T(8,128)(2,1)S(1)}, u32[]{:S(2)}, u32[]{:S(2)}) collective-permute-start(bf16[1280,128]{1,0:T(8,128)(2,1)} %get-tuple-element.23), channel_id=1, source_target_pairs={{0,36},{8,44},{16,52},{24,60},{32,0},{40,8},{48,16},{56,24},{4,32}... | collective-permute-start | bytes 983048 | tf_op jit(solution)/shard_map/ppermute | solution.py:35
  50.1 1.3 copy-start
  51.5 15.0 %copy-start.1 = (bf16[2,64,256]{2,1,0:T(8,128)(2,1)S(1)}, bf16[2,64,256]{2,1,0:T(8,128)(2,1)}, u32[]{:S(2)}) copy-start(bf16[2,64,256]{2,1,0:T(8,128)(2,1)} %get-tuple-element.21) | copy-start | bytes 196612
  51.5 28.8 %all-to-all-start = ((bf16[4,2048,128]{2,1,0:T(8,128)(2,1)}), bf16[4,2048,128]{2,1,0:T(8,128)(2,1)S(1)}, u32[]{:S(2)}, u32[]{:S(2)}) async-start(bf16[4,2048,128]{2,1,0:T(8,128)(2,1)} %copy-done), calls=%async_computation | async-start | bytes 4194304 | tf_op jit(solution)/shard_map/all_to_all | solution.py:22
  56.4 10.1 %collective-permute-start.2 = (bf16[2,64,256]{2,1,0:T(8,128)(2,1)S(1)}, bf16[2,64,256]{2,1,0:T(8,128)(2,1)S(1)}, u32[]{:S(2)}, u32[]{:S(2)}) collective-permute-start(bf16[2,64,256]{2,1,0:T(8,128)(2,1)S(1)} %get-tuple-element.24), channel_id=1, source_target_pairs={{0,36},{8,44},{16,52},{24,60},{32,0},{40,8},{48,16},{56,24},{4,32}... | collective-permute-start | bytes 196616 | tf_op jit(solution)/shard_map/ppermute | solution.py:35
  66.5 15.8 %collective-permute-start.5 = (bf16[4,2,64,256]{3,2,1,0:T(8,128)(2,1)S(1)}, bf16[4,2,64,256]{3,2,1,0:T(8,128)(2,1)S(1)}, u32[]{:S(2)}, u32[]{:S(2)}) collective-permute-start(bf16[4,2,64,256]{3,2,1,0:T(8,128)(2,1)S(1)} %pad_maximum_fusion.same), channel_id=1, source_target_pairs={{0,52},{8,60},{16,0},{24,8},{32,16},{40,24},{48,32},{56,40},{4,48}... | collective-permute-start | bytes 786440 | tf_op jit(solution)/shard_map/ppermute | solution.py:35
  68.4 13.8 %collective-permute-start.4 = (bf16[4,2,64,256]{3,2,1,0:T(8,128)(2,1)S(1)}, bf16[4,2,64,256]{3,2,1,0:T(8,128)(2,1)S(1)}, u32[]{:S(2)}, u32[]{:S(2)}) collective-permute-start(bf16[4,2,64,256]{3,2,1,0:T(8,128)(2,1)S(1)} %pad_maximum_fusion.same), channel_id=1, source_target_pairs={{0,8},{8,16},{16,24},{24,32},{32,40},{40,48},{48,56},{56,4},{4,12}... | collective-permute-start | bytes 786440 | tf_op jit(solution)/shard_map/ppermute | solution.py:35
  71.7 14.9 %collective-permute-start.3 = (bf16[4,2,64,256]{3,2,1,0:T(8,128)(2,1)S(1)}, bf16[4,2,64,256]{3,2,1,0:T(8,128)(2,1)S(1)}, u32[]{:S(2)}, u32[]{:S(2)}) collective-permute-start(bf16[4,2,64,256]{3,2,1,0:T(8,128)(2,1)S(1)} %pad_maximum_fusion.same), channel_id=1, source_target_pairs={{0,60},{8,0},{16,8},{24,16},{32,24},{40,32},{48,40},{56,48},{4,56}... | collective-permute-start | bytes 786440 | tf_op jit(solution)/shard_map/ppermute | solution.py:35
  80.3 7.4 %collective-permute-start.6 = (bf16[4,2048,128]{2,1,0:T(8,128)(2,1)S(1)}, bf16[4,2048,128]{2,1,0:T(8,128)(2,1)S(1)}, u32[]{:S(2)}, u32[]{:S(2)}) collective-permute-start(bf16[4,2048,128]{2,1,0:T(8,128)(2,1)S(1)} %all-to-all-done.block), channel_id=1, source_target_pairs={{0,64},{64,0},{1,65},{65,1},{2,66},{66,2},{3,67},{67,3},{4,68},{68... | collective-permute-start | bytes 6291464 | tf_op jit(solution)/shard_map/ppermute | solution.py:30
  125.6 21.1 %collective-permute-start.7 = (bf16[4,2,64,256]{3,2,1,0:T(8,128)(2,1)S(1)}, bf16[4,2,64,256]{3,2,1,0:T(8,128)(2,1)S(1)}, u32[]{:S(2)}, u32[]{:S(2)}) collective-permute-start(bf16[4,2,64,256]{3,2,1,0:T(8,128)(2,1)S(1)} %get-tuple-element.36), channel_id=1, source_target_pairs={{0,8},{8,16},{16,24},{24,32},{32,40},{40,48},{48,56},{56,4},{4,12}... | collective-permute-start | bytes 786440 | tf_op jit(solution)/shard_map/ppermute | solution.py:35
  127.6 19.2 %collective-permute-start.8 = (bf16[4,2,64,256]{3,2,1,0:T(8,128)(2,1)S(1)}, bf16[4,2,64,256]{3,2,1,0:T(8,128)(2,1)S(1)}, u32[]{:S(2)}, u32[]{:S(2)}) collective-permute-start(bf16[4,2,64,256]{3,2,1,0:T(8,128)(2,1)S(1)} %get-tuple-element.37), channel_id=1, source_target_pairs={{0,60},{8,0},{16,8},{24,16},{32,24},{40,32},{48,40},{56,48},{4,56}... | collective-permute-start | bytes 786440 | tf_op jit(solution)/shard_map/ppermute | solution.py:35
  132.7 10.0 %collective-permute-start.9 = (bf16[2,2,64,256]{3,2,1,0:T(8,128)(2,1)S(1)}, bf16[2,2,64,256]{3,2,1,0:T(8,128)(2,1)S(1)}, u32[]{:S(2)}, u32[]{:S(2)}) collective-permute-start(bf16[2,2,64,256]{3,2,1,0:T(8,128)(2,1)S(1)} %get-tuple-element.38), channel_id=1, source_target_pairs={{0,16},{8,24},{16,32},{24,40},{32,48},{40,56},{48,4},{56,12},{4,20... | collective-permute-start | bytes 393224 | tf_op jit(solution)/shard_map/ppermute | solution.py:35
  134.6 12.1 %collective-permute-start.10 = (bf16[2,2,64,256]{3,2,1,0:T(8,128)(2,1)S(1)}, bf16[2,2,64,256]{3,2,1,0:T(8,128)(2,1)S(1)}, u32[]{:S(2)}, u32[]{:S(2)}) collective-permute-start(bf16[2,2,64,256]{3,2,1,0:T(8,128)(2,1)S(1)} %get-tuple-element.39), channel_id=1, source_target_pairs={{0,52},{8,60},{16,0},{24,8},{32,16},{40,24},{48,32},{56,40},{4,48}... | collective-permute-start | bytes 393224 | tf_op jit(solution)/shard_map/ppermute | solution.py:35

commit v6 on v5

--- a/solution.py
+++ b/solution.py
@@ -134,9 +134,8 @@
     )
 
 
-def own_kernel(same, ahead, behind, far, block, rows, ins, outs, preact, grad):
+def own_kernel(same, ahead, behind, far, ins, outs, rows, preact, grad):
     lay_rows(rows, same, ahead, behind, far)
-    lay_share(block, ins, outs)
     own_preact, own_grad = share_products(rows, ins, outs, lax.axis_index("core"))
     preact[...] = own_preact.astype(BF16)
     grad[...] = own_grad
@@ -213,18 +212,18 @@
     )
     blocks, next_rows, last_rows = call(
         join_kernel, [(4, 2048, 128), (2, 64, 256), (2, 64, 256)], along_z(up, 4), along_z(down, -4),
-        scratch=[pltpu.SemaphoreType.DMA((16,))], space=outside, out_space=outside,
+        scratch=[pltpu.SemaphoreType.DMA((16,))], space=outside, out_space=outside, mib=52,
     )
     blocks = exchange(blocks, "x")
     same = jnp.stack([own, next_rows, along_z(next_rows, -4), last_rows])
     behind, ahead = along_z(same, 1), along_z(same, -1)
     far = along_z(same, -2)
     share = [(1024, 512), (512, 1024)]
-    rows, ins, outs, preact, grad = call(
+    ins, outs = call(lay_share, share, blocks, cost=COST)
+    rows, preact, grad = call(
         own_kernel,
-        [(2, 1024, 256)] + share + [(256, 512), jax.ShapeDtypeStruct((256, 1024), F32)],
-        same, ahead, behind, far, blocks,
-        cost=COST,
+        [(2, 1024, 256), (256, 512), jax.ShapeDtypeStruct((256, 1024), F32)],
+        same, ahead, behind, far, ins, outs,
     )
     other_ins, other_outs, terms = call(
         first_kernel, share + [(4, 2, 256, 256)], rows, swap(blocks, "core"), preact, grad

time: 172 us -> 172 us (level)
    pallas_call x6 -> x7, Pallas kernels: 6.42 us -> 7.68 us  [call(): pl.pallas_call(kernel, out_shape=[jax.ShapeDtypeStruct(shape, BF16) if is...]
where the time goes in v6:
time: 172 us; the launch traced here: 169 us
  blocking collectives  56.6 us (33%)
  waiting for transfers between devices  53.2 us (31%)
  starting transfers between devices  49.8 us (29%)
  Pallas kernels  7.68 us (4%)
    all_to_all x3, blocking collectives, exchange(): return lax.all_to_all(parts, axis, split_axis=0, concat_axis=0, tiled=True)  56.6 us
    ppermute x10, waiting for transfers between devices, along_z(): lax.ppermute(block, ALONG_Z, [(index(z), index((z + distance) % 16)) for...  48.3 us
    ppermute x10, starting transfers between devices, along_z(): lax.ppermute(block, ALONG_Z, [(index(z), index((z + distance) % 16)) for...  43 us
    pallas_call x7, Pallas kernels, call(): pl.pallas_call(kernel, out_shape=[jax.ShapeDtypeStruct(shape, BF16) if is...  7.68 us
    all_to_all x1, starting transfers between devices, exchange(): return lax.all_to_all(parts, axis, split_axis=0, concat_axis=0, tiled=True)  4.91 us
    all_to_all x1, waiting for transfers between devices, exchange(): return lax.all_to_all(parts, axis, split_axis=0, concat_axis=0, tiled=True)  4.84 us
  transfers between devices with their start and end apart: 12, of which 7 were waited for; matrix products, arithmetic and copies ran while one was open for 0% of the time, Pallas kernels for 1%

profile of v6, /device:TPU:6, one launch (start us, length us, event | category | flops | bytes accessed | tf_op | source)
XLA Modules:
  0.0 169.0 jit_solution(13207542975606777390)
XLA Ops:
  0.6 2.1 %shard_map.68 = (bf16[2,64,256]{2,1,0:T(8,128)(2,1)}, bf16[1280,128]{1,0:T(8,128)(2,1)}, bf16[1280,128]{1,0:T(8,128)(2,1)}) custom-call(bf16[64,256]{1,0:T(8,128)(2,1)} %bitcast.21, bf16[64,256]{1,0:T(8,128)(2,1)} %bitcast.22, s32[1,256]{1,0:T(1,128)} %bitcast.23, bf16[512,256]{1,0:T(8,128)(2,1)} %refs_3_.1, bf16[64,2048]{1,0:T(8,128)(2,1)} %bitcast.18), custom_call_target="tpu_custom_call" | custom-call | tf_op jit(solution)/shard_map/pallas_call | solution.py:193
  2.7 9.1 %collective-permute-start = (bf16[1280,128]{1,0:T(8,128)(2,1)}, bf16[1280,128]{1,0:T(8,128)(2,1)S(1)}, u32[]{:S(2)}, u32[]{:S(2)}) collective-permute-start(bf16[1280,128]{1,0:T(8,128)(2,1)} %get-tuple-element.22), channel_id=1, source_target_pairs={{0,32},{8,40},{16,48},{24,56},{32,4},{40,12},{48,20},{56,28},{4,36... | collective-permute-start | bytes 983048 | tf_op jit(solution)/shard_map/ppermute | solution.py:35
  11.8 5.6 %collective-permute-start.1 = (bf16[1280,128]{1,0:T(8,128)(2,1)}, bf16[1280,128]{1,0:T(8,128)(2,1)S(1)}, u32[]{:S(2)}, u32[]{:S(2)}) collective-permute-start(bf16[1280,128]{1,0:T(8,128)(2,1)} %get-tuple-element.23), channel_id=1, source_target_pairs={{0,36},{8,44},{16,52},{24,60},{32,0},{40,8},{48,16},{56,24},{4,32}... | collective-permute-start | bytes 983048 | tf_op jit(solution)/shard_map/ppermute | solution.py:35
  17.4 10.7 %collective-permute-done.below = bf16[1280,128]{1,0:T(8,128)(2,1)S(1)} collective-permute-done((bf16[1280,128]{1,0:T(8,128)(2,1)}, bf16[1280,128]{1,0:T(8,128)(2,1)S(1)}, u32[]{:S(2)}, u32[]{:S(2)}) %collective-permute-start) | collective-permute-done | bytes 327712 | tf_op jit(solution)/shard_map/ppermute | solution.py:35
  28.1 21.7 %collective-permute-done.1.above = bf16[1280,128]{1,0:T(8,128)(2,1)S(1)} collective-permute-done((bf16[1280,128]{1,0:T(8,128)(2,1)}, bf16[1280,128]{1,0:T(8,128)(2,1)S(1)}, u32[]{:S(2)}, u32[]{:S(2)}) %collective-permute-start.1) | collective-permute-done | bytes 327712 | tf_op jit(solution)/shard_map/ppermute | solution.py:35
  49.8 1.5 shard_map.69
  51.3 0.0 copy-start
  51.3 4.9 %all-to-all-start = ((bf16[4,2048,128]{2,1,0:T(8,128)(2,1)}), bf16[4,2048,128]{2,1,0:T(8,128)(2,1)S(1)}, u32[]{:S(2)}, u32[]{:S(2)}) async-start(bf16[4,2048,128]{2,1,0:T(8,128)(2,1)} %get-tuple-element.26), calls=%async_computation | async-start | bytes 4194304 | tf_op jit(solution)/shard_map/all_to_all | solution.py:22
  56.2 4.4 %collective-permute-start.2 = (bf16[2,64,256]{2,1,0:T(8,128)(2,1)S(1)}, bf16[2,64,256]{2,1,0:T(8,128)(2,1)S(1)}, u32[]{:S(2)}, u32[]{:S(2)}) collective-permute-start(bf16[2,64,256]{2,1,0:T(8,128)(2,1)S(1)} %get-tuple-element.24), channel_id=1, source_target_pairs={{0,36},{8,44},{16,52},{24,60},{32,0},{40,8},{48,16},{56,24},{4,32}... | collective-permute-start | bytes 196616 | tf_op jit(solution)/shard_map/ppermute | solution.py:35
  60.6 5.7 %collective-permute-done.2 = bf16[2,64,256]{2,1,0:T(8,128)(2,1)S(1)} collective-permute-done((bf16[2,64,256]{2,1,0:T(8,128)(2,1)S(1)}, bf16[2,64,256]{2,1,0:T(8,128)(2,1)S(1)}, u32[]{:S(2)}, u32[]{:S(2)}) %collective-permute-start.2) | collective-permute-done | bytes 65568 | tf_op jit(solution)/shard_map/ppermute | solution.py:35
  66.3 0.0 copy-done
  66.3 1.9 %collective-permute-start.5 = (bf16[4,2,64,256]{3,2,1,0:T(8,128)(2,1)S(1)}, bf16[4,2,64,256]{3,2,1,0:T(8,128)(2,1)S(1)}, u32[]{:S(2)}, u32[]{:S(2)}) collective-permute-start(bf16[4,2,64,256]{3,2,1,0:T(8,128)(2,1)S(1)} %pad_maximum_fusion.same), channel_id=1, source_target_pairs={{0,52},{8,60},{16,0},{24,8},{32,16},{40,24},{48,32},{56,40},{4,48}... | collective-permute-start | bytes 786440 | tf_op jit(solution)/shard_map/ppermute | solution.py:35
  68.2 3.3 %collective-permute-start.4 = (bf16[4,2,64,256]{3,2,1,0:T(8,128)(2,1)S(1)}, bf16[4,2,64,256]{3,2,1,0:T(8,128)(2,1)S(1)}, u32[]{:S(2)}, u32[]{:S(2)}) collective-permute-start(bf16[4,2,64,256]{3,2,1,0:T(8,128)(2,1)S(1)} %pad_maximum_fusion.same), channel_id=1, source_target_pairs={{0,8},{8,16},{16,24},{24,32},{32,40},{40,48},{48,56},{56,4},{4,12}... | collective-permute-start | bytes 786440 | tf_op jit(solution)/shard_map/ppermute | solution.py:35
  71.5 3.8 %collective-permute-start.3 = (bf16[4,2,64,256]{3,2,1,0:T(8,128)(2,1)S(1)}, bf16[4,2,64,256]{3,2,1,0:T(8,128)(2,1)S(1)}, u32[]{:S(2)}, u32[]{:S(2)}) collective-permute-start(bf16[4,2,64,256]{3,2,1,0:T(8,128)(2,1)S(1)} %pad_maximum_fusion.same), channel_id=1, source_target_pairs={{0,60},{8,0},{16,8},{24,16},{32,24},{40,32},{48,40},{56,48},{4,56}... | collective-permute-start | bytes 786440 | tf_op jit(solution)/shard_map/ppermute | solution.py:35
  75.3 4.8 %all-to-all-done.block = bf16[4,2048,128]{2,1,0:T(8,128)(2,1)S(1)} async-done(((bf16[4,2048,128]{2,1,0:T(8,128)(2,1)}), bf16[4,2048,128]{2,1,0:T(8,128)(2,1)S(1)}, u32[]{:S(2)}, u32[]{:S(2)}) %all-to-all-start) | async-done | bytes 2097184 | tf_op jit(solution)/shard_map/all_to_all | solution.py:22
  80.1 1.9 %collective-permute-start.6 = (bf16[4,2048,128]{2,1,0:T(8,128)(2,1)S(1)}, bf16[4,2048,128]{2,1,0:T(8,128)(2,1)S(1)}, u32[]{:S(2)}, u32[]{:S(2)}) collective-permute-start(bf16[4,2048,128]{2,1,0:T(8,128)(2,1)S(1)} %all-to-all-done.block), channel_id=1, source_target_pairs={{0,64},{64,0},{1,65},{65,1},{2,66},{66,2},{3,67},{67,3},{4,68},{68... | collective-permute-start | bytes 6291464 | tf_op jit(solution)/shard_map/ppermute | solution.py:30
  82.0 0.4 shard_map.70
  82.4 0.0 collective-permute-done.5.far
  82.4 0.0 collective-permute-done.4.behind
  82.5 3.9 %collective-permute-done.3.ahead = bf16[4,2,64,256]{3,2,1,0:T(8,128)(2,1)S(1)} collective-permute-done((bf16[4,2,64,256]{3,2,1,0:T(8,128)(2,1)S(1)}, bf16[4,2,64,256]{3,2,1,0:T(8,128)(2,1)S(1)}, u32[]{:S(2)}, u32[]{:S(2)}) %collective-permute-start.3) | collective-permute-done | bytes 262176 | tf_op jit(solution)/shard_map/ppermute | solution.py:35
  86.4 0.8 shard_map.71
  87.2 0.0 collective-permute-done.6.block
  87.2 1.1 shard_map.72
  88.3 19.1 %all_to_all.20.terms = bf16[4,2,256,256]{3,2,1,0:T(8,128)(2,1)S(1)} all-to-all(bf16[4,2,256,256]{3,2,1,0:T(8,128)(2,1)S(1)} %get-tuple-element.32), channel_id=1, replica_groups=mesh['x'=4,'core'=2,'quad'=2,'place'=4,'half'=2,'y'=4] {'y'}, dimensions={0} | all-to-all | bytes 2097152 | tf_op jit(solution)/shard_map/all_to_all | solution.py:22
  107.4 0.3 shard_map.73
  107.7 16.0 %all_to_all.21.hidden = bf16[4,2,256,256]{3,2,1,0:T(8,128)(2,1)S(1)} all-to-all(bf16[4,2,256,256]{3,2,1,0:T(8,128)(2,1)S(1)} %shard_map.73), channel_id=1, replica_groups=mesh['x'=4,'core'=2,'quad'=2,'place'=4,'half'=2,'y'=4] {'y'}, dimensions={0} | all-to-all | bytes 2097152 | tf_op jit(solution)/shard_map/all_to_all | solution.py:22
  123.7 1.5 shard_map.74
  125.2 1.9 %collective-permute-start.7 = (bf16[4,2,64,256]{3,2,1,0:T(8,128)(2,1)S(1)}, bf16[4,2,64,256]{3,2,1,0:T(8,128)(2,1)S(1)}, u32[]{:S(2)}, u32[]{:S(2)}) collective-permute-start(bf16[4,2,64,256]{3,2,1,0:T(8,128)(2,1)S(1)} %get-tuple-element.36), channel_id=1, source_target_pairs={{0,8},{8,16},{16,24},{24,32},{32,40},{40,48},{48,56},{56,4},{4,12}... | collective-permute-start | bytes 786440 | tf_op jit(solution)/shard_map/ppermute | solution.py:35
  127.1 5.1 %collective-permute-start.8 = (bf16[4,2,64,256]{3,2,1,0:T(8,128)(2,1)S(1)}, bf16[4,2,64,256]{3,2,1,0:T(8,128)(2,1)S(1)}, u32[]{:S(2)}, u32[]{:S(2)}) collective-permute-start(bf16[4,2,64,256]{3,2,1,0:T(8,128)(2,1)S(1)} %get-tuple-element.37), channel_id=1, source_target_pairs={{0,60},{8,0},{16,8},{24,16},{32,24},{40,32},{48,40},{56,48},{4,56}... | collective-permute-start | bytes 786440 | tf_op jit(solution)/shard_map/ppermute | solution.py:35
  132.3 1.9 %collective-permute-start.9 = (bf16[2,2,64,256]{3,2,1,0:T(8,128)(2,1)S(1)}, bf16[2,2,64,256]{3,2,1,0:T(8,128)(2,1)S(1)}, u32[]{:S(2)}, u32[]{:S(2)}) collective-permute-start(bf16[2,2,64,256]{3,2,1,0:T(8,128)(2,1)S(1)} %get-tuple-element.38), channel_id=1, source_target_pairs={{0,16},{8,24},{16,32},{24,40},{32,48},{40,56},{48,4},{56,12},{4,20... | collective-permute-start | bytes 393224 | tf_op jit(solution)/shard_map/ppermute | solution.py:35
  134.2 6.0 %collective-permute-start.10 = (bf16[2,2,64,256]{3,2,1,0:T(8,128)(2,1)S(1)}, bf16[2,2,64,256]{3,2,1,0:T(8,128)(2,1)S(1)}, u32[]{:S(2)}, u32[]{:S(2)}) collective-permute-start(bf16[2,2,64,256]{3,2,1,0:T(8,128)(2,1)S(1)} %get-tuple-element.39), channel_id=1, source_target_pairs={{0,52},{8,60},{16,0},{24,8},{32,16},{40,24},{48,32},{56,40},{4,48}... | collective-permute-start | bytes 393224 | tf_op jit(solution)/shard_map/ppermute | solution.py:35
  140.2 2.0 %collective-permute-done.9 = bf16[2,2,64,256]{3,2,1,0:T(8,128)(2,1)S(1)} collective-permute-done((bf16[2,2,64,256]{3,2,1,0:T(8,128)(2,1)S(1)}, bf16[2,2,64,256]{3,2,1,0:T(8,128)(2,1)S(1)}, u32[]{:S(2)}, u32[]{:S(2)}) %collective-permute-start.9) | collective-permute-done | bytes 131104 | tf_op jit(solution)/shard_map/ppermute | solution.py:35
  142.3 4.4 %collective-permute-done.10 = bf16[2,2,64,256]{3,2,1,0:T(8,128)(2,1)S(1)} collective-permute-done((bf16[2,2,64,256]{3,2,1,0:T(8,128)(2,1)S(1)}, bf16[2,2,64,256]{3,2,1,0:T(8,128)(2,1)S(1)}, u32[]{:S(2)}, u32[]{:S(2)}) %collective-permute-start.10) | collective-permute-done | bytes 131104 | tf_op jit(solution)/shard_map/ppermute | solution.py:35
  146.6 0.0 collective-permute-done.7
  146.6 0.0 collective-permute-done.8
  146.6 0.1 add_convert_fusion
  146.8 21.5 %all_to_all.22 = bf16[4,2,64,256]{3,2,1,0:T(8,128)(2,1)S(1)} all-to-all(bf16[4,2,64,256]{3,2,1,0:T(8,128)(2,1)S(1)} %add_convert_fusion), channel_id=1, replica_groups=mesh['x'=4,'core'=2,'quad'=2,'place'=4,'half'=2,'y'=4] {'half','quad'}, dimensions={0} | all-to-all | bytes 524288 | tf_op jit(solution)/shard_map/all_to_all | solution.py:22
  168.4 0.6 slice_bitcast_fusion
  (3 shorter events, 0.1 us)
Async XLA Ops:
  2.7 25.4 %collective-permute-start = (bf16[1280,128]{1,0:T(8,128)(2,1)}, bf16[1280,128]{1,0:T(8,128)(2,1)S(1)}, u32[]{:S(2)}, u32[]{:S(2)}) collective-permute-start(bf16[1280,128]{1,0:T(8,128)(2,1)} %get-tuple-element.22), channel_id=1, source_target_pairs={{0,32},{8,40},{16,48},{24,56},{32,4},{40,12},{48,20},{56,28},{4,36... | collective-permute-start | bytes 983048 | tf_op jit(solution)/shard_map/ppermute | solution.py:35
  11.8 37.9 %collective-permute-start.1 = (bf16[1280,128]{1,0:T(8,128)(2,1)}, bf16[1280,128]{1,0:T(8,128)(2,1)S(1)}, u32[]{:S(2)}, u32[]{:S(2)}) collective-permute-start(bf16[1280,128]{1,0:T(8,128)(2,1)} %get-tuple-element.23), channel_id=1, source_target_pairs={{0,36},{8,44},{16,52},{24,60},{32,0},{40,8},{48,16},{56,24},{4,32}... | collective-permute-start | bytes 983048 | tf_op jit(solution)/shard_map/ppermute | solution.py:35
  51.3 15.0 %copy-start = (bf16[2,64,256]{2,1,0:T(8,128)(2,1)S(1)}, bf16[2,64,256]{2,1,0:T(8,128)(2,1)}, u32[]{:S(2)}) copy-start(bf16[2,64,256]{2,1,0:T(8,128)(2,1)} %get-tuple-element.21) | copy-start | bytes 196612
  51.3 28.8 %all-to-all-start = ((bf16[4,2048,128]{2,1,0:T(8,128)(2,1)}), bf16[4,2048,128]{2,1,0:T(8,128)(2,1)S(1)}, u32[]{:S(2)}, u32[]{:S(2)}) async-start(bf16[4,2048,128]{2,1,0:T(8,128)(2,1)} %get-tuple-element.26), calls=%async_computation | async-start | bytes 4194304 | tf_op jit(solution)/shard_map/all_to_all | solution.py:22
  56.2 10.1 %collective-permute-start.2 = (bf16[2,64,256]{2,1,0:T(8,128)(2,1)S(1)}, bf16[2,64,256]{2,1,0:T(8,128)(2,1)S(1)}, u32[]{:S(2)}, u32[]{:S(2)}) collective-permute-start(bf16[2,64,256]{2,1,0:T(8,128)(2,1)S(1)} %get-tuple-element.24), channel_id=1, source_target_pairs={{0,36},{8,44},{16,52},{24,60},{32,0},{40,8},{48,16},{56,24},{4,32}... | collective-permute-start | bytes 196616 | tf_op jit(solution)/shard_map/ppermute | solution.py:35
  66.3 16.1 %collective-permute-start.5 = (bf16[4,2,64,256]{3,2,1,0:T(8,128)(2,1)S(1)}, bf16[4,2,64,256]{3,2,1,0:T(8,128)(2,1)S(1)}, u32[]{:S(2)}, u32[]{:S(2)}) collective-permute-start(bf16[4,2,64,256]{3,2,1,0:T(8,128)(2,1)S(1)} %pad_maximum_fusion.same), channel_id=1, source_target_pairs={{0,52},{8,60},{16,0},{24,8},{32,16},{40,24},{48,32},{56,40},{4,48}... | collective-permute-start | bytes 786440 | tf_op jit(solution)/shard_map/ppermute | solution.py:35
  68.2 14.2 %collective-permute-start.4 = (bf16[4,2,64,256]{3,2,1,0:T(8,128)(2,1)S(1)}, bf16[4,2,64,256]{3,2,1,0:T(8,128)(2,1)S(1)}, u32[]{:S(2)}, u32[]{:S(2)}) collective-permute-start(bf16[4,2,64,256]{3,2,1,0:T(8,128)(2,1)S(1)} %pad_maximum_fusion.same), channel_id=1, source_target_pairs={{0,8},{8,16},{16,24},{24,32},{32,40},{40,48},{48,56},{56,4},{4,12}... | collective-permute-start | bytes 786440 | tf_op jit(solution)/shard_map/ppermute | solution.py:35
  71.5 14.9 %collective-permute-start.3 = (bf16[4,2,64,256]{3,2,1,0:T(8,128)(2,1)S(1)}, bf16[4,2,64,256]{3,2,1,0:T(8,128)(2,1)S(1)}, u32[]{:S(2)}, u32[]{:S(2)}) collective-permute-start(bf16[4,2,64,256]{3,2,1,0:T(8,128)(2,1)S(1)} %pad_maximum_fusion.same), channel_id=1, source_target_pairs={{0,60},{8,0},{16,8},{24,16},{32,24},{40,32},{48,40},{56,48},{4,56}... | collective-permute-start | bytes 786440 | tf_op jit(solution)/shard_map/ppermute | solution.py:35
  80.1 7.1 %collective-permute-start.6 = (bf16[4,2048,128]{2,1,0:T(8,128)(2,1)S(1)}, bf16[4,2048,128]{2,1,0:T(8,128)(2,1)S(1)}, u32[]{:S(2)}, u32[]{:S(2)}) collective-permute-start(bf16[4,2048,128]{2,1,0:T(8,128)(2,1)S(1)} %all-to-all-done.block), channel_id=1, source_target_pairs={{0,64},{64,0},{1,65},{65,1},{2,66},{66,2},{3,67},{67,3},{4,68},{68... | collective-permute-start | bytes 6291464 | tf_op jit(solution)/shard_map/ppermute | solution.py:30
  125.2 21.4 %collective-permute-start.7 = (bf16[4,2,64,256]{3,2,1,0:T(8,128)(2,1)S(1)}, bf16[4,2,64,256]{3,2,1,0:T(8,128)(2,1)S(1)}, u32[]{:S(2)}, u32[]{:S(2)}) collective-permute-start(bf16[4,2,64,256]{3,2,1,0:T(8,128)(2,1)S(1)} %get-tuple-element.36), channel_id=1, source_target_pairs={{0,8},{8,16},{16,24},{24,32},{32,40},{40,48},{48,56},{56,4},{4,12}... | collective-permute-start | bytes 786440 | tf_op jit(solution)/shard_map/ppermute | solution.py:35
  127.1 19.5 %collective-permute-start.8 = (bf16[4,2,64,256]{3,2,1,0:T(8,128)(2,1)S(1)}, bf16[4,2,64,256]{3,2,1,0:T(8,128)(2,1)S(1)}, u32[]{:S(2)}, u32[]{:S(2)}) collective-permute-start(bf16[4,2,64,256]{3,2,1,0:T(8,128)(2,1)S(1)} %get-tuple-element.37), channel_id=1, source_target_pairs={{0,60},{8,0},{16,8},{24,16},{32,24},{40,32},{48,40},{56,48},{4,56}... | collective-permute-start | bytes 786440 | tf_op jit(solution)/shard_map/ppermute | solution.py:35
  132.3 10.0 %collective-permute-start.9 = (bf16[2,2,64,256]{3,2,1,0:T(8,128)(2,1)S(1)}, bf16[2,2,64,256]{3,2,1,0:T(8,128)(2,1)S(1)}, u32[]{:S(2)}, u32[]{:S(2)}) collective-permute-start(bf16[2,2,64,256]{3,2,1,0:T(8,128)(2,1)S(1)} %get-tuple-element.38), channel_id=1, source_target_pairs={{0,16},{8,24},{16,32},{24,40},{32,48},{40,56},{48,4},{56,12},{4,20... | collective-permute-start | bytes 393224 | tf_op jit(solution)/shard_map/ppermute | solution.py:35
  134.2 12.4 %collective-permute-start.10 = (bf16[2,2,64,256]{3,2,1,0:T(8,128)(2,1)S(1)}, bf16[2,2,64,256]{3,2,1,0:T(8,128)(2,1)S(1)}, u32[]{:S(2)}, u32[]{:S(2)}) collective-permute-start(bf16[2,2,64,256]{3,2,1,0:T(8,128)(2,1)S(1)} %get-tuple-element.39), channel_id=1, source_target_pairs={{0,52},{8,60},{16,0},{24,8},{32,16},{40,24},{48,32},{56,40},{4,48}... | collective-permute-start | bytes 393224 | tf_op jit(solution)/shard_map/ppermute | solution.py:35
